TPU v7x, 32 devices: a whole 2x2x4 slice. The times are simulated.
32 devices in a mesh: parts: 2 (over x), kv: 2 (over core), req: 8 (over z, y).
Axes of the slice: x: 2, y: 2, z: 4, core: 2. Of those that a mesh axis runs over, the one named last changes fastest.
Arguments:
- hidden: bfloat16 [16, 16384], P(('parts', 'req')), parts along dimension 0, may hold values from -6 to 6
- norm_gain: float32 [16384], replicated, may hold values from 0.1 to 1.9
- w_query: bfloat16 [16384, 2, 2048], P('req', 'kv'), may hold values from -0.046875 to 0.046875
- w_keyval: bfloat16 [16384, 2, 256], P('req', 'kv'), may hold values from -0.046875 to 0.046875
- w_out: bfloat16 [2, 2048, 16384], P('kv', None, 'req'), may hold values from -0.125 to 0.125
- cache: bfloat16 [2, 384, 512, 256], P('kv', ('parts', 'req')), parts along dimension 1, may hold values from -140 to 140
- slot_request: int32 [384], P(('parts', 'req')), parts along dimension 0, may hold values from -1 to 7, as said below
- slot_block: int32 [384], P(('parts', 'req')), parts along dimension 0, may hold values from -1 to 63
- cache_lengths: int32 [16], P('parts'), parts along dimension 0, may hold values from 1 to 32768, as said below
Outputs:
- attention_out: bfloat16 [16, 16384], P(('parts', 'req')), parts along dimension 0
There are 2 independent parts, one for each index of `parts`. A program takes and returns all parts, laid end to end along the dimension named above; an argument that names none is the same for every part. Nothing has to cross between parts.
Inputs may be any that keep to these rules, and one draw needn't show every extreme that they name: Slot p of a device's 24 slots holds block slot_block[p] of request slot_request[p], or is empty (-1 in both). Every block of request r, that is ceil(cache_lengths[r] / 512) blocks, stands in exactly one slot of the pool; on each device the occupied slots come first. `cache_lengths`: one request has exactly 32768 cached tokens; every other one has at most 8192.
All inputs are finite; a program needn't handle non-finite values.
Results may differ from a plain program's by a relative error of at most 0.007.
The roundings to bfloat16 on the way count: a program that leaves them out, or rounds other values in their place, can miss the bound.
Values may be sent and summed in bfloat16 or wider, within the bound.
No kernel may reach another device: no remote copies, remote signals or barrier semaphores. Data moves between devices by JAX's collectives and lax.ppermute only.
A program may use at most 64 MiB of HBM per device.

v0:
```python
import jax
import jax.numpy as jnp
from jax import lax
from jax.sharding import PartitionSpec as P


def joined(x, axis, combine):
    everything = jax.tree.map(lambda part: lax.all_gather(part, axis), x)
    leading = jax.tree.map(lambda part: part[0], everything)

    def turn(k, so_far):
        return combine(so_far, jax.tree.map(lambda part: part[k], everything))

    return lax.fori_loop(1, lax.axis_size(axis), turn, leading)


def combine(first, second):
    top_score = jnp.maximum(first[0], second[0])
    first_factor = jnp.exp(first[0] - top_score)
    second_factor = jnp.exp(second[0] - top_score)
    merged_sum = first[1] * first_factor + second[1] * second_factor
    merged_out = first[2] * first_factor[..., None] + second[2] * second_factor[..., None]
    return (top_score, merged_sum, merged_out)


def finish(top_part, sum_part, out_part, own_query, own_key, own_value, score_scale):
    own_score = (
        jnp.einsum("rhd,rd->rh", own_query, own_key, preferred_element_type=jnp.float32)
        * score_scale
    )
    top_score = jnp.maximum(top_part, own_score)
    old_factor = jnp.exp(top_part - top_score)
    own_factor = jnp.exp(own_score - top_score)
    denominator = own_factor + old_factor * sum_part
    summed = (
        own_factor[:, :, None] * own_value.astype(jnp.float32)[:, None, :]
        + old_factor[:, :, None] * out_part
    )
    return (summed / denominator[:, :, None]).astype(jnp.bfloat16)


def on_device(
    hidden, norm_gain, w_query, w_keyval, w_out, cache, slot_request, slot_block, cache_lengths
):
    highest = lax.Precision.HIGHEST
    activations = hidden.astype(jnp.float32)
    normed = (
        activations
        * lax.rsqrt(jnp.mean(activations * activations, axis=1, keepdims=True) + 1e-05)
        * norm_gain
    ).astype(jnp.bfloat16)
    columns = lax.all_to_all(normed, "req", split_axis=1, concat_axis=0, tiled=True)
    feature_rows = columns.shape[1]
    requests = columns.shape[0]
    query_weight = w_query.reshape(feature_rows, -1)
    pair_weight = w_keyval.reshape(feature_rows, -1)
    head_width = query_weight.shape[1]
    head_dim = pair_weight.shape[1] // 2
    head_count = head_width // head_dim
    score_scale = head_dim ** (-0.5)
    query_sum, pair_sum = lax.psum(
        (
            jnp.dot(columns, query_weight, preferred_element_type=jnp.float32),
            jnp.dot(columns, pair_weight, preferred_element_type=jnp.float32),
        ),
        "req",
    )
    queries = query_sum.astype(jnp.bfloat16)
    key_value = pair_sum.astype(jnp.bfloat16)
    new_key = key_value[:, :head_dim]
    new_value = key_value[:, head_dim:]
    slot_count = slot_request.shape[0]
    block_tokens = cache.shape[2]
    request_ids = jnp.arange(requests, dtype=jnp.int32)
    owner_hot = slot_request[:, None] == request_ids[None, :]
    slot_query = (
        jnp.dot(owner_hot.astype(jnp.bfloat16), queries, preferred_element_type=jnp.float32)
        .astype(jnp.bfloat16)
        .reshape(slot_count, head_count, head_dim)
    )
    slot_length = jnp.sum(jnp.where(owner_hot, cache_lengths[None, :], 0), axis=1)
    positions = (
        slot_block[:, None] * block_tokens + jnp.arange(block_tokens, dtype=jnp.int32)[None, :]
    )
    live_tokens = (slot_request >= 0)[:, None] & (positions < slot_length[:, None])
    block_cache = cache[0]
    block_keys = block_cache[:, :, :head_dim]
    block_values = block_cache[:, :, head_dim:]
    scores = (
        jnp.einsum("shd,std->sht", slot_query, block_keys, preferred_element_type=jnp.float32)
        * score_scale
    )
    masked = jnp.where(live_tokens[:, None, :], scores, -1e30)
    block_max = jnp.max(masked, axis=2)
    weights = jnp.where(live_tokens[:, None, :], jnp.exp(masked - block_max[:, :, None]), 0.0)
    block_sum = jnp.sum(weights, axis=2)
    block_out = jnp.einsum(
        "sht,std->shd",
        weights.astype(jnp.bfloat16),
        block_values,
        preferred_element_type=jnp.float32,
    )
    device_max = jnp.max(jnp.where(owner_hot[:, :, None], block_max[:, None, :], -1e30), axis=0)
    factor = jnp.where(
        owner_hot[:, :, None], jnp.exp(block_max[:, None, :] - device_max[None, :, :]), 0.0
    )
    device_sum = jnp.einsum("srh,sh->rh", factor, block_sum, precision=highest)
    device_out = jnp.einsum("srh,shd->rhd", factor, block_out, precision=highest)
    top_part, sum_part, out_part = joined((device_max, device_sum, device_out), "req", combine)
    attended = finish(
        top_part,
        sum_part,
        out_part,
        queries.reshape(requests, head_count, head_dim),
        new_key,
        new_value,
        score_scale,
    )
    flattened = attended.reshape(requests, head_width)
    projected = jnp.dot(flattened, w_out[0], preferred_element_type=jnp.float32)
    summed_heads = lax.psum(projected, "kv").astype(jnp.bfloat16)
    return lax.all_to_all(summed_heads, "req", split_axis=0, concat_axis=1, tiled=True)


def solution(mesh):
    placed = (
        P(("parts", "req"), None),
        P(),
        P("req", "kv", None),
        P("req", "kv", None),
        P("kv", None, "req"),
        P("kv", ("parts", "req"), None, None),
        P(("parts", "req")),
        P(("parts", "req")),
        P("parts"),
    )
    return jax.shard_map(
        on_device, mesh=mesh, in_specs=placed, out_specs=P(("parts", "req"), None), check_vma=False
    )
```

profile of v0, /device:TPU:0, one launch (start us, length us, event | category | flops | bytes accessed | tf_op | source)
XLA Modules:
  0.0 178.1 jit_solution(14820383546395036889)
XLA Ops:
  0.0 0.0 copy-start
  0.0 1.7 multiply_reduce_fusion.1
  2.4 1.0 multiply_convert_fusion
  3.3 0.6 broadcast.61
  3.9 0.9 reduce.3
  4.8 0.6 reshape.128
  5.4 7.3 %all-to-all-start = ((bf16[8,2,1024]{2,1,0:T(2,128)(2,1)}), bf16[8,2,1024]{2,1,0:T(2,128)(2,1)S(1)}, u32[]{:S(2)}, u32[]{:S(2)}) async-start(bf16[8,2,1024]{2,1,0:T(2,128)(2,1)} %reshape.128), calls=%async_computation | async-start | bytes 65536 | tf_op jit(solution)/shard_map/all_to_all | solution.py:52
  12.7 0.7 broadcast_multiply_fusion
  13.4 0.7 broadcast_compare_fusion
  14.0 0.8 select_reduce_fusion.1
  14.8 0.1 fusion.28
  14.9 0.7 iota_compare_fusion
  15.5 3.9 %all-to-all-done = bf16[8,2,1024]{2,1,0:T(2,128)(2,1)S(1)} async-done(((bf16[8,2,1024]{2,1,0:T(2,128)(2,1)}), bf16[8,2,1024]{2,1,0:T(2,128)(2,1)S(1)}, u32[]{:S(2)}, u32[]{:S(2)}) %all-to-all-start) | async-done | bytes 32800 | tf_op jit(solution)/shard_map/all_to_all | solution.py:52
  19.4 0.0 copy-done
  19.4 0.2 fusion.19
  19.7 0.0 copy-start.1
  19.7 4.6 %fusion.6 = f32[8,2048]{1,0:T(8,128)S(1)} fusion(bf16[2048,1,2048]{2,0,1:T(8,128)(2,1)} %param.13, bf16[1,8,2048]{2,0,1:T(2,128)(2,1)S(1)} %bitcast.75), kind=kOutput, calls=%fused_computation.12 | convolution fusion | flops 67108864 | bytes 8486912 | tf_op jit(solution)/shard_map/dot_general | solution.py:63
  24.3 34.6 %all-reduce = (bf16[8,2048]{1,0:T(8,128)(2,1)S(1)}, bf16[8,256]{1,0:T(8,128)(2,1)S(1)}) all-reduce(f32[8,2048]{1,0:T(8,128)S(1)} %fusion.6, f32[8,256]{1,0:T(8,128)S(1)} %fusion.19), channel_id=1, replica_groups=mesh['parts'=2,'kv'=2,'req'=8] {'req'}, use_global_device_ids=true, to_apply=%region_1.0 | all-reduce | flops 18432 | bytes 110592 | tf_op jit(solution)/shard_map/psum | solution.py:61
  58.9 0.0 copy-done.1
  58.9 0.2 fusion.18
  59.1 2.9 %fusion.52 = (f32[24,16]{1,0:T(8,128)S(1)}, f32[24,16,512]{2,1,0:T(8,128)S(1)}) fusion(bf16[24,16,128]{2,1,0:T(8,128)(2,1)S(1)} %bitcast.73, bf16[24,512,256]{2,1,0:T(8,128)(2,1)} %bitcast.71, pred[24,512]{1,0:T(8,128)(4,1)S(1)} %fusion.28), kind=kOutput, calls=%fused_computation.71 | convolution fusion | flops 50921088 | bytes 4044288 | tf_op jit(solution)/shard_map/shd,std->sht/dot_general | solution.py:90
  62.0 0.1 copy.27
  62.1 0.3 fusion.22
  62.4 2.5 %fusion.8 = f32[24,16,128]{2,1,0:T(8,128)S(1)} fusion(bf16[24,512,256]{2,1,0:T(8,128)(2,1)} %bitcast.72, f32[24,16,512]{2,1,0:T(8,128)S(1)} %get-tuple-element.240, f32[24,16]{1,0:T(8,128)S(1)} %get-tuple-element.239, pred[24,512]{1,0:T(8,128)(4,1)S(1)} %fusion.28), kind=kOutput, calls=%fused_computation.14 | convolution fusion | flops 50921472 | bytes 4142592 | tf_op jit(solution)/shard_map/sht,std->shd/dot_general | solution.py:97
  64.9 0.1 select_reduce_fusion
  65.0 0.1 copy.28
  65.1 0.4 convolution_bitcast_fusion
  65.5 0.1 copy.44
  65.5 0.2 multiply_reduce_fusion
  65.7 0.1 copy.41
  65.8 30.4 %all-gather.1 = f32[64,16]{1,0:T(8,128)S(1)} all-gather(f32[8,16]{1,0:T(8,128)S(1)} %bitcast.83), channel_id=3, replica_groups=mesh['parts'=2,'kv'=2,'req'=8] {'req'}, dimensions={0}, use_global_device_ids=true | all-gather | bytes 4608 | tf_op jit(solution)/shard_map/all_gather | solution.py:8
  96.2 30.4 %all-gather = f32[64,16]{1,0:T(8,128)S(1)} all-gather(f32[8,16]{1,0:T(8,128)S(1)} %copy.28), channel_id=2, replica_groups=mesh['parts'=2,'kv'=2,'req'=8] {'req'}, dimensions={0}, use_global_device_ids=true | all-gather | bytes 4608 | tf_op jit(solution)/shard_map/all_gather | solution.py:8
  126.6 31.2 %all-gather.2 = f32[64,16,128]{2,0,1:T(8,128)S(1)} all-gather(f32[8,16,128]{2,0,1:T(8,128)S(1)} %convolution_bitcast_fusion), channel_id=4, replica_groups=mesh['parts'=2,'kv'=2,'req'=8] {'req'}, dimensions={0}, use_global_device_ids=true | all-gather | bytes 589824 | tf_op jit(solution)/shard_map/all_gather | solution.py:8
  157.8 1.3 while.19
  157.9 0.1 fusion.58
  158.1 0.1 fusion.58
  158.3 0.1 fusion.58
  158.5 0.1 fusion.58
  158.6 0.1 fusion.58
  158.8 0.1 fusion.58
  159.0 0.1 fusion.58
  159.1 0.1 fusion.33
  159.3 0.1 fusion.38
  159.4 4.6 %fusion.4 = f32[8,2048]{1,0:T(8,128)S(1)} fusion(bf16[1,2048,2048]{2,1,0:T(8,128)(2,1)} %param.15, bf16[1,8,16,128]{3,2,1,0:T(8,128)(2,1)S(1)} %fusion.38), kind=kOutput, calls=%fused_computation.10 | convolution fusion | flops 67108864 | bytes 8486912 | tf_op jit(solution)/shard_map/dot_general | solution.py:120
  164.0 3.6 %psum.23 = bf16[8,2048]{1,0:T(8,128)(2,1)S(1)} all-reduce(f32[8,2048]{1,0:T(8,128)S(1)} %fusion.4), channel_id=1, replica_groups=mesh['parts'=2,'kv'=2,'req'=8] {'kv'}, use_global_device_ids=true, to_apply=%region_9.10 | all-reduce | flops 16384 | bytes 98304 | tf_op jit(solution)/shard_map/psum | solution.py:121
  167.6 0.7 reduce.4
  168.3 9.1 %all_to_all.32 = bf16[8,2,1024]{2,1,0:T(2,128)(2,1)S(1)} all-to-all(bf16[8,2,1024]{2,1,0:T(2,128)(2,1)S(1)} %reshape.130), channel_id=1, replica_groups=mesh['parts'=2,'kv'=2,'req'=8] {'req'}, dimensions={0} | all-to-all | bytes 65536 | tf_op jit(solution)/shard_map/all_to_all | solution.py:122
  177.4 0.7 reshape.131
  (23 shorter events, 0.4 us)
Async XLA Ops:
  0.0 19.4 %copy-start = (bf16[2048,1,256]{2,0,1:T(8,128)(2,1)S(1)}, bf16[2048,1,256]{2,0,1:T(8,128)(2,1)}, u32[]{:S(2)}) copy-start(bf16[2048,1,256]{2,0,1:T(8,128)(2,1)} %param.14) | copy-start | bytes 3145732
  5.4 14.0 %all-to-all-start = ((bf16[8,2,1024]{2,1,0:T(2,128)(2,1)}), bf16[8,2,1024]{2,1,0:T(2,128)(2,1)S(1)}, u32[]{:S(2)}, u32[]{:S(2)}) async-start(bf16[8,2,1024]{2,1,0:T(2,128)(2,1)} %reshape.128), calls=%async_computation | async-start | bytes 65536 | tf_op jit(solution)/shard_map/all_to_all | solution.py:52
  19.7 39.2 %copy-start.1 = (s32[24]{0:T(128)S(1)}, s32[24]{0:T(128)}, u32[]{:S(2)}) copy-start(s32[24]{0:T(128)} %param.17) | copy-start | bytes 292
where the time goes:
time: 179 us; the launch traced here: 178 us
  blocking collectives  139 us (78%)
  matrix products  15.5 us (9%)
  other arithmetic  8.65 us (5%)
  starting transfers between devices  7.28 us (4%)
  waiting for transfers between devices  3.86 us (2%)
  local copies, waits for them, and re-layouts  2.39 us (1%)
    all_gather x3, blocking collectives, joined(): everything = jax.tree.map(lambda part: lax.all_gather(part, axis), x)  92 us
    psum x1, blocking collectives, on_device(): lax.psum((jnp.dot(columns, query_weight, preferred_element_type=jnp.float...  34.6 us
    all_to_all x1, blocking collectives, on_device(): lax.all_to_all(summed_heads, 'req', split_axis=0, concat_axis=1, tiled=True)  9.06 us
    all_to_all x1, starting transfers between devices, on_device(): lax.all_to_all(normed, 'req', split_axis=1, concat_axis=0, tiled=True)  7.28 us
    dot_general x1, matrix products, on_device(): jnp.dot(columns, query_weight, preferred_element_type=jnp.float32)  4.59 us
    dot_general x1, matrix products, on_device(): projected = jnp.dot(flattened, w_out[0], preferred_element_type=jnp.float32)  4.57 us
    all_to_all x1, waiting for transfers between devices, on_device(): lax.all_to_all(normed, 'req', split_axis=1, concat_axis=0, tiled=True)  3.86 us
    psum x1, blocking collectives, on_device(): summed_heads = lax.psum(projected, 'kv').astype(jnp.bfloat16)  3.61 us
  transfers between devices with their start and end apart: 1, of which 1 were waited for; matrix products, arithmetic and copies ran while one was open for 2% of the time, Pallas kernels for 0%

commit v1 on v0

v1 whole, which is shorter than its diff:
```python
import functools

import jax
import jax.numpy as jnp
from jax import lax
from jax.experimental import pallas as pl
from jax.experimental.pallas import tpu as pltpu
from jax.sharding import PartitionSpec as P

LANES = 128
EMPTY = -1e30
F32 = jnp.float32
BF16 = jnp.bfloat16
VMEM = pl.BlockSpec(memory_space=pltpu.VMEM)
SMEM = pl.BlockSpec(memory_space=pltpu.SMEM)
MIB = 1024 * 1024


def norm_kernel(hidden_ref, gain_ref, out_ref, rows):
    count = rows.shape[0]
    for row in range(count):
        rows[row : row + 1, :] = hidden_ref[:, row * LANES : (row + 1) * LANES].astype(F32)
    x = rows[...]
    mean = jnp.sum(jnp.sum(x * x, axis=0, keepdims=True), axis=1, keepdims=True) / (count * LANES)
    out_ref[...] = (x * lax.rsqrt(mean + 1e-05) * gain_ref[...]).astype(BF16)


def project_kernel(x_ref, query_ref, pair_ref, out_ref):
    x = x_ref[...].astype(F32)
    x = jnp.concatenate([x[:, chunk, :] for chunk in range(x.shape[1])], axis=1).astype(BF16)
    width = query_ref.shape[1]
    step = 512
    for at in range(0, width, step):
        out_ref[:, at : at + step] = jnp.dot(
            x, query_ref[:, at : at + step], preferred_element_type=F32
        )
    out_ref[:, width:] = jnp.dot(x, pair_ref[...], preferred_element_type=F32)


def attend_kernel(
    me_ref, owner_ref, block_ref, length_ref, mine_ref, other_ref, cache_ref, out_ref,
    wide, query, new_key, new_value, top, total, summed,
):
    requests = mine_ref.shape[0]
    slots, tokens, lanes = cache_ref.shape
    dim = lanes // 2
    heads = (mine_ref.shape[1] - lanes) // dim
    scale = dim ** (-0.5)
    rows = requests * heads
    for head in range(heads):
        at = slice(head * dim, (head + 1) * dim)
        wide[pl.ds(head, requests, stride=heads), :] = mine_ref[:, at] + other_ref[:, at]
    query[...] = wide[...].astype(BF16)
    for new, start in ((new_key, heads * dim), (new_value, heads * dim + dim)):
        at = slice(start, start + dim)
        new[...] = (mine_ref[:, at] + other_ref[:, at]).astype(BF16).astype(F32)

    me = me_ref[0]
    mine = pl.ds(pl.multiple_of(me * heads, heads), heads)
    own_key = new_key[pl.ds(me, 1), :]
    own_value = new_value[pl.ds(me, 1), :]
    own_score = (
        jnp.sum(query[mine, :].astype(F32) * own_key, axis=1, keepdims=True) * scale
    )
    top[...] = jnp.full(top.shape, EMPTY, F32)
    total[...] = jnp.zeros(total.shape, F32)
    summed[...] = jnp.zeros(summed.shape, F32)
    top[mine, :] = jnp.broadcast_to(own_score, (heads, dim))

    token = lax.broadcasted_iota(jnp.int32, (heads, tokens), 1)
    places = []
    maxima = []
    sums = []
    outs = []
    for slot in range(slots):
        owner = owner_ref[slot]
        used = owner >= 0
        source = jnp.maximum(owner, 0)
        live = jnp.where(used, length_ref[source] - block_ref[slot] * tokens, 0)
        scores = (
            lax.dot_general(
                query[pl.ds(pl.multiple_of(source * heads, heads), heads), :],
                cache_ref[slot, :, :dim],
                (((1,), (1,)), ((), ())),
                preferred_element_type=F32,
            )
            * scale
        )
        masked = jnp.where(token < live, scores, EMPTY)
        block_max = jnp.max(masked, axis=1, keepdims=True)
        weights = jnp.exp(masked - block_max)
        block_sum = jnp.sum(weights, axis=1, keepdims=True)
        block_out = jnp.dot(
            weights.astype(BF16), cache_ref[slot, :, dim:], preferred_element_type=F32
        )
        places.append(pl.ds(pl.multiple_of(jnp.where(used, owner, requests) * heads, heads), heads))
        maxima.append(jnp.broadcast_to(block_max, (heads, dim)))
        sums.append(jnp.broadcast_to(block_sum, (heads, dim)))
        outs.append(block_out)
    for place, block_max in zip(places, maxima):
        top[place, :] = jnp.maximum(top[place, :], block_max)
    for place, block_max, block_sum, block_out in zip(places, maxima, sums, outs):
        factor = jnp.exp(block_max - top[place, :])
        total[place, :] = total[place, :] + factor * block_sum
        summed[place, :] = summed[place, :] + factor * block_out
    own_factor = jnp.exp(own_score - top[mine, :])
    total[mine, :] = total[mine, :] + own_factor
    summed[mine, :] = summed[mine, :] + own_factor * own_value

    out_ref[:dim, :] = summed[:rows, :].T
    out_ref[dim : dim + 1, :] = top[:rows, :].T[:1, :]
    out_ref[dim + 1 : dim + 2, :] = total[:rows, :].T[:1, :]
    out_ref[dim + 2 :, :] = jnp.zeros((out_ref.shape[0] - dim - 2, rows), F32)


def merged(first_ref, second_ref):
    dim = LANES
    first_top = first_ref[dim : dim + 1, :]
    second_top = second_ref[dim : dim + 1, :]
    top = jnp.maximum(first_top, second_top)
    first_factor = jnp.exp(first_top - top)
    second_factor = jnp.exp(second_top - top)
    total = (
        first_ref[dim + 1 : dim + 2, :] * first_factor
        + second_ref[dim + 1 : dim + 2, :] * second_factor
    )
    summed = first_ref[:dim, :] * first_factor + second_ref[:dim, :] * second_factor
    return top, total, summed


def merge_kernel(first_ref, second_ref, out_ref):
    dim = LANES
    top, total, summed = merged(first_ref, second_ref)
    out_ref[:dim, :] = summed
    out_ref[dim : dim + 1, :] = top
    out_ref[dim + 1 : dim + 2, :] = total
    out_ref[dim + 2 :, :] = jnp.zeros((out_ref.shape[0] - dim - 2, out_ref.shape[1]), F32)


def output_kernel(first_ref, second_ref, weight_ref, out_ref, rows):
    _, total, summed = merged(first_ref, second_ref)
    rows[...] = (summed / total).T
    heads = weight_ref.shape[0] // LANES
    requests = rows.shape[0] // heads
    x = jnp.concatenate(
        [rows[pl.ds(head, requests, stride=heads), :] for head in range(heads)], axis=1
    ).astype(BF16)
    width = weight_ref.shape[1]
    chunks = width // LANES
    step = min(512, width)
    for at in range(0, width, step):
        y = jnp.dot(x, weight_ref[:, at : at + step], preferred_element_type=F32)
        for chunk in range(step // LANES):
            part = y[:, chunk * LANES : (chunk + 1) * LANES]
            for copy in range(out_ref.shape[0]):
                out_ref[copy, pl.ds(at // LANES + chunk, requests, stride=chunks), :] = part


def call(kernel, shape, dtype, in_specs, scratch=(), limit=4 * MIB, flops=0, moved=0):
    return pl.pallas_call(
        kernel,
        out_shape=jax.ShapeDtypeStruct(shape, dtype),
        in_specs=in_specs,
        out_specs=VMEM,
        scratch_shapes=list(scratch),
        compiler_params=pltpu.CompilerParams(vmem_limit_bytes=limit),
        cost_estimate=pl.CostEstimate(flops=flops, bytes_accessed=moved, transcendentals=0),
    )


def exchanged(x, distance, size):
    return lax.ppermute(x, "req", [(place, place ^ distance) for place in range(size)])


def on_device(
    sizes, hidden, norm_gain, w_query, w_keyval, w_out, cache, slot_request, slot_block, cache_lengths
):
    requests = sizes["req"]
    features = hidden.shape[1]
    feature_rows = features // requests
    query_weight = w_query.reshape(feature_rows, -1)
    pair_weight = w_keyval.reshape(feature_rows, -1)
    head_width = query_weight.shape[1]
    lanes = pair_weight.shape[1]
    dim = lanes // 2
    heads = head_width // dim
    rows = requests * heads
    slots, tokens = cache.shape[1:3]

    normed = call(
        norm_kernel, (features // LANES, LANES), BF16, [VMEM, VMEM],
        [pltpu.VMEM((features // LANES, LANES), F32)],
    )(hidden, norm_gain.reshape(features // LANES, LANES))
    columns = lax.all_to_all(
        normed.reshape(requests, feature_rows // LANES, LANES), "req", 0, 0, tiled=True
    )
    sums = call(
        project_kernel, (requests, head_width + lanes), F32, [VMEM] * 3, limit=16 * MIB,
        flops=2 * requests * feature_rows * (head_width + lanes),
        moved=2 * feature_rows * (head_width + lanes),
    )(columns, query_weight, pair_weight)
    distance = 1
    while distance < requests:
        other = exchanged(sums, distance, requests)
        distance *= 2
        if distance < requests:
            sums = sums + other

    me = lax.axis_index("req").astype(jnp.int32).reshape(1)
    part = call(
        attend_kernel, (dim + 8, rows), F32, [SMEM] * 4 + [VMEM] * 3,
        [
            pltpu.VMEM((rows, dim), F32),
            pltpu.VMEM((rows, dim), BF16),
            pltpu.VMEM((requests, dim), F32),
            pltpu.VMEM((requests, dim), F32),
            pltpu.VMEM((rows + heads, dim), F32),
            pltpu.VMEM((rows + heads, dim), F32),
            pltpu.VMEM((rows + heads, dim), F32),
        ],
        limit=16 * MIB,
        flops=2 * slots * tokens * heads * lanes,
        moved=2 * slots * tokens * lanes,
    )(me, slot_request, slot_block, cache_lengths, sums, other, cache[0])
    distance = 1
    while distance < requests:
        other = exchanged(part, distance, requests)
        distance *= 2
        if distance < requests:
            part = call(merge_kernel, part.shape, F32, [VMEM] * 2)(part, other)

    columns_out = w_out.shape[2]
    projected = call(
        output_kernel, (sizes["kv"], requests * columns_out // LANES, LANES), F32, [VMEM] * 3,
        [pltpu.VMEM((rows, dim), F32)],
        limit=16 * MIB,
        flops=2 * requests * head_width * columns_out,
        moved=2 * head_width * columns_out,
    )(part, other, w_out[0])
    terms = lax.all_to_all(
        projected.reshape(sizes["kv"] * requests, columns_out // LANES, LANES),
        ("kv", "req"), 0, 0, tiled=True,
    )
    terms = terms.reshape(sizes["kv"], -1)
    return jnp.sum(terms, axis=0, keepdims=True).astype(BF16)


def solution(mesh):
    placed = (
        P(("parts", "req"), None),
        P(),
        P("req", "kv", None),
        P("req", "kv", None),
        P("kv", None, "req"),
        P("kv", ("parts", "req"), None, None),
        P(("parts", "req")),
        P(("parts", "req")),
        P("parts"),
    )
    return jax.shard_map(
        functools.partial(on_device, dict(mesh.shape)),
        mesh=mesh, in_specs=placed, out_specs=P(("parts", "req"), None), check_vma=False,
    )
```

time: 179 us -> 76.9 us (0.43)
  blocking collectives: 139 us -> 24 us
  waiting for transfers between devices: 3.86 us -> 27.1 us
  matrix products: 15.5 us -> 0 us
  local copies, waits for them, and re-layouts: 2.39 us -> 13.2 us
  Pallas kernels: 0 us -> 9.39 us
  other arithmetic: 8.65 us -> 0.19 us
  starting transfers between devices: 7.28 us -> 2.47 us
    all_gather x3 -> x0, blocking collectives: 92 us -> none  [joined(): everything = jax.tree.map(lambda part: lax.all_gather(part, axis), x)]
    psum x2 -> x0, blocking collectives: 38.2 us -> none  [the longest x1 34.6 us: on_device(): lax.psum((jnp.dot(columns, query_weight, preferred_element_type=jnp.float...]
    ppermute x0 -> x6, waiting for transfers between devices: none -> 27.1 us  [exchanged(): lax.ppermute(x, 'req', [(place, place ^ distance) for place in range(size)])]
    dot_general x8 -> x0, matrix products: 15.5 us -> none  [the longest x1 4.59 us: on_device(): jnp.dot(columns, query_weight, preferred_element_type=jnp.float32)]
    all_to_all x1 -> x2, blocking collectives: 9.06 us -> 24 us  [the longest x1 13.8 us: on_device(): lax.all_to_all(normed.reshape(requests, feature_rows // LANES, LANES), 'r...]
    unnamed x11 -> x18, local copies, waits for them, and re-layouts: 2.03 us -> 12.5 us
    pallas_call x0 -> x6, Pallas kernels: none -> 9.39 us  [the longest x1 6.57 us: on_device(): call(attend_kernel, (dim + 8, rows), F32, [SMEM] * 4 + [VMEM] * 3, [pltpu...]
    all_to_all x1 -> x0, starting transfers between devices: 7.28 us -> none  [on_device(): lax.all_to_all(normed, 'req', split_axis=1, concat_axis=0, tiled=True)]
  transfers between devices with their start and end apart: 1 -> 6, of which waited for: 1 -> 6; matrix products, arithmetic and copies ran while one was open for 2% -> 0% of each run, Pallas kernels for 0% -> 0%
where the time goes in v1:
time: 76.9 us; the launch traced here: 76.5 us
  waiting for transfers between devices  27.1 us (35%)
  blocking collectives  24 us (31%)
  local copies, waits for them, and re-layouts  13.2 us (17%)
  Pallas kernels  9.39 us (12%)
  starting transfers between devices  2.47 us (3%)
    ppermute x6, waiting for transfers between devices, exchanged(): lax.ppermute(x, 'req', [(place, place ^ distance) for place in range(size)])  27.1 us
    all_to_all x1, blocking collectives, on_device(): lax.all_to_all(normed.reshape(requests, feature_rows // LANES, LANES), 'r...  13.8 us
    unnamed x18, local copies, waits for them, and re-layouts  12.5 us
    all_to_all x1, blocking collectives, on_device(): lax.all_to_all(projected.reshape(sizes['kv'] * requests, columns_out // L...  10.2 us
    pallas_call x1, Pallas kernels, on_device(): call(attend_kernel, (dim + 8, rows), F32, [SMEM] * 4 + [VMEM] * 3, [pltpu...  6.57 us
    ppermute x6, starting transfers between devices, exchanged(): lax.ppermute(x, 'req', [(place, place ^ distance) for place in range(size)])  2.47 us
  transfers between devices with their start and end apart: 6, of which 6 were waited for; matrix products, arithmetic and copies ran while one was open for 0% of the time, Pallas kernels for 0%

profile of v1, /device:TPU:0, one launch (start us, length us, event | category | flops | bytes accessed | tf_op | source)
XLA Modules:
  0.0 76.5 jit_solution(6304717498644026033)
XLA Ops:
  0.0 0.0 copy-start.8
  0.0 0.0 copy-start.7
  0.0 0.0 copy-start.6
  0.0 0.0 copy-start.4
  0.0 0.9 %copy-done.4 = bf16[1,16384]{1,0:T(2,128)(2,1)S(1)} copy-done((bf16[1,16384]{1,0:T(2,128)(2,1)S(1)}, bf16[1,16384]{1,0:T(2,128)(2,1)}, u32[]{:S(2)}) %copy-start.4) | copy-done | bytes 32792
  0.9 0.0 copy-start.5
  0.9 0.8 %copy-done.5 = f32[16384]{0:T(1024)S(1)} copy-done((f32[16384]{0:T(1024)S(1)}, f32[16384]{0:T(1024)}, u32[]{:S(2)}) %copy-start.5) | copy-done | bytes 65560
  1.7 0.2 shard_map.91
  1.9 13.8 %all_to_all.10.x_ref = bf16[8,16,128]{2,1,0:T(8,128)(2,1)S(1)} all-to-all(bf16[8,16,128]{2,1,0:T(8,128)(2,1)S(1)} %bitcast.13), channel_id=1, replica_groups=mesh['parts'=2,'kv'=2,'req'=8] {'req'}, dimensions={0} | all-to-all | bytes 65536 | tf_op jit(solution)/shard_map/all_to_all | solution.py:194
  15.6 0.0 copy-start.1
  15.7 3.4 %copy-done.1 = bf16[2048,1,2048]{2,0,1:T(8,128)(2,1)S(1)} copy-done((bf16[2048,1,2048]{2,0,1:T(8,128)(2,1)S(1)}, bf16[2048,1,2048]{2,0,1:T(8,128)(2,1)}, u32[]{:S(2)}) %copy-start.1) | copy-done | bytes 8388632
  19.0 0.0 copy-start.3
  19.0 1.2 %copy-done.3 = bf16[2048,1,256]{2,0,1:T(8,128)(2,1)S(1)} copy-done((bf16[2048,1,256]{2,0,1:T(8,128)(2,1)S(1)}, bf16[2048,1,256]{2,0,1:T(8,128)(2,1)}, u32[]{:S(2)}) %copy-start.3) | copy-done | bytes 1048600
  20.3 1.3 %shard_map.92 = f32[8,2304]{1,0:T(8,128)S(1)} custom-call(bf16[8,16,128]{2,1,0:T(8,128)(2,1)S(1)} %all_to_all.10.x_ref, bf16[2048,2048]{1,0:T(8,128)(2,1)S(1)} %bitcast.9, bf16[2048,256]{1,0:T(8,128)(2,1)S(1)} %bitcast.11), custom_call_target="tpu_custom_call" | custom-call | flops 75497472 | bytes 9437184 | tf_op jit(solution)/shard_map/pallas_call | solution.py:197
  21.6 0.5 collective-permute-start
  22.1 3.9 %collective-permute-done = f32[8,2304]{1,0:T(8,128)S(1)} collective-permute-done((f32[8,2304]{1,0:T(8,128)S(1)}, f32[8,2304]{1,0:T(8,128)S(1)}, u32[]{:S(2)}, u32[]{:S(2)}) %collective-permute-start) | collective-permute-done | bytes 73760 | tf_op jit(solution)/shard_map/ppermute | solution.py:172
  26.0 0.5 collective-permute-start.1
  26.4 4.3 %collective-permute-done.1 = f32[8,2304]{1,0:T(8,128)S(1)} collective-permute-done((f32[8,2304]{1,0:T(8,128)S(1)}, f32[8,2304]{1,0:T(8,128)S(1)}, u32[]{:S(2)}, u32[]{:S(2)}) %collective-permute-start.1) | collective-permute-done | bytes 73760 | tf_op jit(solution)/shard_map/ppermute | solution.py:172
  30.7 0.7 collective-permute-start.2
  31.4 5.4 %collective-permute-done.2.other_ref = f32[8,2304]{1,0:T(8,128)S(1)} collective-permute-done((f32[8,2304]{1,0:T(8,128)S(1)}, f32[8,2304]{1,0:T(8,128)S(1)}, u32[]{:S(2)}, u32[]{:S(2)}) %collective-permute-start.2) | collective-permute-done | bytes 73760 | tf_op jit(solution)/shard_map/ppermute | solution.py:172
  36.8 0.0 copy-done.8
  36.8 0.0 copy-done.7
  36.8 0.0 copy-done.6
  36.8 0.0 copy-start.2
  36.8 2.8 %copy-done.2 = bf16[1,24,512,256]{3,2,1,0:T(8,128)(2,1)S(1)} copy-done((bf16[1,24,512,256]{3,2,1,0:T(8,128)(2,1)S(1)}, bf16[1,24,512,256]{3,2,1,0:T(8,128)(2,1)}, u32[]{:S(2)}) %copy-start.2) | copy-done | bytes 6291480
  39.6 6.6 %shard_map.93.first_ref = f32[136,128]{1,0:T(8,128)S(1)} custom-call(s32[1]{0:T(128)} %bitcast.me_ref, s32[24]{0:T(128)S(1)} %copy-done.6, s32[24]{0:T(128)S(1)} %copy-done.7, s32[8]{0:T(128)S(1)} %copy-done.8, f32[8,2304]{1,0:T(8,128)S(1)} %add.7.mine_ref, f32[8,2304]{1,0:T(8,128)S(1)} %collective-permute-done.2.other_ref, bf16[24,512,256]{2,1,0:T(8,128)(2,1)S(1)} %bitcast.10), custom_call_target="tpu_custom_call" | custom-call | flops 100663296 | bytes 6291456 | tf_op jit(solution)/shard_map/pallas_call | solution.py:210
  46.2 0.5 collective-permute-start.3
  46.7 3.9 %collective-permute-done.3.second_ref = f32[136,128]{1,0:T(8,128)S(1)} collective-permute-done((f32[136,128]{1,0:T(8,128)S(1)}, f32[136,128]{1,0:T(8,128)S(1)}, u32[]{:S(2)}, u32[]{:S(2)}) %collective-permute-start.3) | collective-permute-done | bytes 69664 | tf_op jit(solution)/shard_map/ppermute | solution.py:172
  50.6 0.2 collective-permute-start.4
  50.8 4.1 %collective-permute-done.4.second_ref = f32[136,128]{1,0:T(8,128)S(1)} collective-permute-done((f32[136,128]{1,0:T(8,128)S(1)}, f32[136,128]{1,0:T(8,128)S(1)}, u32[]{:S(2)}, u32[]{:S(2)}) %collective-permute-start.4) | collective-permute-done | bytes 69664 | tf_op jit(solution)/shard_map/ppermute | solution.py:172
  55.0 0.1 collective-permute-start.5
  55.1 5.5 %collective-permute-done.5.second_ref = f32[136,128]{1,0:T(8,128)S(1)} collective-permute-done((f32[136,128]{1,0:T(8,128)S(1)}, f32[136,128]{1,0:T(8,128)S(1)}, u32[]{:S(2)}, u32[]{:S(2)}) %collective-permute-start.5) | collective-permute-done | bytes 69664 | tf_op jit(solution)/shard_map/ppermute | solution.py:172
  60.6 0.0 copy-start
  60.6 3.4 %copy-done = bf16[1,2048,2048]{2,1,0:T(8,128)(2,1)S(1)} copy-done((bf16[1,2048,2048]{2,1,0:T(8,128)(2,1)S(1)}, bf16[1,2048,2048]{2,1,0:T(8,128)(2,1)}, u32[]{:S(2)}) %copy-start) | copy-done | bytes 8388632
  64.0 1.3 %shard_map.96 = f32[2,128,128]{2,1,0:T(8,128)S(1)} custom-call(f32[136,128]{1,0:T(8,128)S(1)} %shard_map.95.first_ref, f32[136,128]{1,0:T(8,128)S(1)} %collective-permute-done.5.second_ref, bf16[2048,2048]{1,0:T(8,128)(2,1)S(1)} %bitcast.8), custom_call_target="tpu_custom_call" | custom-call | flops 67108864 | bytes 8388608 | tf_op jit(solution)/shard_map/pallas_call | solution.py:233
  65.3 10.2 %all_to_all.11 = f32[16,16,128]{2,1,0:T(8,128)S(1)} all-to-all(f32[16,16,128]{2,1,0:T(8,128)S(1)} %bitcast.12), channel_id=1, replica_groups=mesh['parts'=2,'kv'=2,'req'=8] {'kv','req'}, dimensions={0} | all-to-all | bytes 262144 | tf_op jit(solution)/shard_map/all_to_all | solution.py:240
  75.5 0.1 reshape.36
  75.6 0.2 reduce_sum.9
  75.8 0.7 convert_element_type.15
  (4 shorter events, 0.1 us)
Async XLA Ops:
  0.0 36.8 %copy-start.8 = (s32[8]{0:T(128)S(1)}, s32[8]{0:T(128)}, u32[]{:S(2)}) copy-start(s32[8]{0:T(128)} %length_ref.1) | copy-start | bytes 100
  0.0 36.8 %copy-start.7 = (s32[24]{0:T(128)S(1)}, s32[24]{0:T(128)}, u32[]{:S(2)}) copy-start(s32[24]{0:T(128)} %block_ref.1) | copy-start | bytes 292
  0.0 36.8 %copy-start.6 = (s32[24]{0:T(128)S(1)}, s32[24]{0:T(128)}, u32[]{:S(2)}) copy-start(s32[24]{0:T(128)} %owner_ref.1) | copy-start | bytes 292
  0.0 0.9 %copy-start.4 = (bf16[1,16384]{1,0:T(2,128)(2,1)S(1)}, bf16[1,16384]{1,0:T(2,128)(2,1)}, u32[]{:S(2)}) copy-start(bf16[1,16384]{1,0:T(2,128)(2,1)} %hidden_ref.1) | copy-start | bytes 98308
  0.9 0.8 %copy-start.5 = (f32[16384]{0:T(1024)S(1)}, f32[16384]{0:T(1024)}, u32[]{:S(2)}) copy-start(f32[16384]{0:T(1024)} %param.10) | copy-start | bytes 196612
  15.6 3.4 %copy-start.1 = (bf16[2048,1,2048]{2,0,1:T(8,128)(2,1)S(1)}, bf16[2048,1,2048]{2,0,1:T(8,128)(2,1)}, u32[]{:S(2)}) copy-start(bf16[2048,1,2048]{2,0,1:T(8,128)(2,1)} %param.11) | copy-start | bytes 25165828
  19.0 1.2 %copy-start.3 = (bf16[2048,1,256]{2,0,1:T(8,128)(2,1)S(1)}, bf16[2048,1,256]{2,0,1:T(8,128)(2,1)}, u32[]{:S(2)}) copy-start(bf16[2048,1,256]{2,0,1:T(8,128)(2,1)} %param.12) | copy-start | bytes 3145732
  21.6 4.4 %collective-permute-start = (f32[8,2304]{1,0:T(8,128)S(1)}, f32[8,2304]{1,0:T(8,128)S(1)}, u32[]{:S(2)}, u32[]{:S(2)}) collective-permute-start(f32[8,2304]{1,0:T(8,128)S(1)} %shard_map.92), channel_id=1, source_target_pairs={{0,1},{1,0},{2,3},{3,2},{4,5},{5,4},{6,7},{7,6},{8,9},{9,8},{10,11... | collective-permute-start | bytes 221192 | tf_op jit(solution)/shard_map/ppermute | solution.py:172
  26.0 4.7 %collective-permute-start.1 = (f32[8,2304]{1,0:T(8,128)S(1)}, f32[8,2304]{1,0:T(8,128)S(1)}, u32[]{:S(2)}, u32[]{:S(2)}) collective-permute-start(f32[8,2304]{1,0:T(8,128)S(1)} %add.6), channel_id=1, source_target_pairs={{0,2},{1,3},{2,0},{3,1},{4,6},{5,7},{6,4},{7,5},{8,10},{9,11},{10,... | collective-permute-start | bytes 221192 | tf_op jit(solution)/shard_map/ppermute | solution.py:172
  30.7 6.1 %collective-permute-start.2 = (f32[8,2304]{1,0:T(8,128)S(1)}, f32[8,2304]{1,0:T(8,128)S(1)}, u32[]{:S(2)}, u32[]{:S(2)}) collective-permute-start(f32[8,2304]{1,0:T(8,128)S(1)} %add.7.mine_ref), channel_id=1, source_target_pairs={{0,4},{1,5},{2,6},{3,7},{4,0},{5,1},{6,2},{7,3},{8,12},{9,13},{10,... | collective-permute-start | bytes 221192 | tf_op jit(solution)/shard_map/ppermute | solution.py:172
  36.8 2.8 %copy-start.2 = (bf16[1,24,512,256]{3,2,1,0:T(8,128)(2,1)S(1)}, bf16[1,24,512,256]{3,2,1,0:T(8,128)(2,1)}, u32[]{:S(2)}) copy-start(bf16[1,24,512,256]{3,2,1,0:T(8,128)(2,1)} %param.14) | copy-start | bytes 18874372
  46.2 4.4 %collective-permute-start.3 = (f32[136,128]{1,0:T(8,128)S(1)}, f32[136,128]{1,0:T(8,128)S(1)}, u32[]{:S(2)}, u32[]{:S(2)}) collective-permute-start(f32[136,128]{1,0:T(8,128)S(1)} %shard_map.93.first_ref), channel_id=1, source_target_pairs={{0,1},{1,0},{2,3},{3,2},{4,5},{5,4},{6,7},{7,6},{8,9},{9,8},{10,11... | collective-permute-start | bytes 208904 | tf_op jit(solution)/shard_map/ppermute | solution.py:172
  50.6 4.4 %collective-permute-start.4 = (f32[136,128]{1,0:T(8,128)S(1)}, f32[136,128]{1,0:T(8,128)S(1)}, u32[]{:S(2)}, u32[]{:S(2)}) collective-permute-start(f32[136,128]{1,0:T(8,128)S(1)} %shard_map.94.first_ref), channel_id=1, source_target_pairs={{0,2},{1,3},{2,0},{3,1},{4,6},{5,7},{6,4},{7,5},{8,10},{9,11},{10,... | collective-permute-start | bytes 208904 | tf_op jit(solution)/shard_map/ppermute | solution.py:172
  55.0 5.6 %collective-permute-start.5 = (f32[136,128]{1,0:T(8,128)S(1)}, f32[136,128]{1,0:T(8,128)S(1)}, u32[]{:S(2)}, u32[]{:S(2)}) collective-permute-start(f32[136,128]{1,0:T(8,128)S(1)} %shard_map.95.first_ref), channel_id=1, source_target_pairs={{0,4},{1,5},{2,6},{3,7},{4,0},{5,1},{6,2},{7,3},{8,12},{9,13},{10,... | collective-permute-start | bytes 208904 | tf_op jit(solution)/shard_map/ppermute | solution.py:172
  60.6 3.4 %copy-start = (bf16[1,2048,2048]{2,1,0:T(8,128)(2,1)S(1)}, bf16[1,2048,2048]{2,1,0:T(8,128)(2,1)}, u32[]{:S(2)}) copy-start(bf16[1,2048,2048]{2,1,0:T(8,128)(2,1)} %param.13) | copy-start | bytes 25165828

commit v2 on v1

--- a/solution.py
+++ b/solution.py
@@ -16,18 +16,23 @@
 MIB = 1024 * 1024
 
 
-def norm_kernel(hidden_ref, gain_ref, out_ref, rows):
-    count = rows.shape[0]
-    for row in range(count):
-        rows[row : row + 1, :] = hidden_ref[:, row * LANES : (row + 1) * LANES].astype(F32)
-    x = rows[...]
-    mean = jnp.sum(jnp.sum(x * x, axis=0, keepdims=True), axis=1, keepdims=True) / (count * LANES)
-    out_ref[...] = (x * lax.rsqrt(mean + 1e-05) * gain_ref[...]).astype(BF16)
-
-
-def project_kernel(x_ref, query_ref, pair_ref, out_ref):
-    x = x_ref[...].astype(F32)
-    x = jnp.concatenate([x[:, chunk, :] for chunk in range(x.shape[1])], axis=1).astype(BF16)
+def spread_kernel(hidden_ref, out_ref):
+    for row in range(out_ref.shape[0]):
+        out_ref[row : row + 1, :] = hidden_ref[:, row * LANES : (row + 1) * LANES].astype(F32)
+
+
+def scale_kernel(x_ref, out_ref):
+    x = x_ref[...]
+    mean = jnp.sum(jnp.sum(x * x, axis=0, keepdims=True), axis=1, keepdims=True) / x.size
+    out_ref[...] = x * lax.rsqrt(mean + 1e-05)
+
+
+def project_kernel(x_ref, gain_ref, query_ref, pair_ref, out_ref):
+    chunks = x_ref.shape[1]
+    me = lax.axis_index("req").astype(jnp.int32)
+    gain = gain_ref[pl.ds(pl.multiple_of(me * chunks, chunks), chunks), :]
+    x = x_ref[...] * gain[None]
+    x = jnp.concatenate([x[:, chunk, :] for chunk in range(chunks)], axis=1).astype(BF16)
     width = query_ref.shape[1]
     step = 512
     for at in range(0, width, step):
@@ -38,7 +43,7 @@
 
 
 def attend_kernel(
-    me_ref, owner_ref, block_ref, length_ref, mine_ref, other_ref, cache_ref, out_ref,
+    owner_ref, block_ref, length_ref, mine_ref, other_ref, cache_ref, out_ref,
     wide, query, new_key, new_value, top, total, summed,
 ):
     requests = mine_ref.shape[0]
@@ -55,7 +60,7 @@
         at = slice(start, start + dim)
         new[...] = (mine_ref[:, at] + other_ref[:, at]).astype(BF16).astype(F32)
 
-    me = me_ref[0]
+    me = lax.axis_index("req").astype(jnp.int32)
     mine = pl.ds(pl.multiple_of(me * heads, heads), heads)
     own_key = new_key[pl.ds(me, 1), :]
     own_value = new_value[pl.ds(me, 1), :]
@@ -68,41 +73,40 @@
     top[mine, :] = jnp.broadcast_to(own_score, (heads, dim))
 
     token = lax.broadcasted_iota(jnp.int32, (heads, tokens), 1)
-    places = []
-    maxima = []
-    sums = []
-    outs = []
+    owners = [owner_ref[slot] for slot in range(slots)]
+    sources = [jnp.maximum(owner, 0) for owner in owners]
+    lives = [
+        jnp.where(owners[slot] >= 0, length_ref[sources[slot]] - block_ref[slot] * tokens, 0)
+        for slot in range(slots)
+    ]
+    places = [
+        pl.ds(pl.multiple_of(jnp.where(owner >= 0, owner, requests) * heads, heads), heads)
+        for owner in owners
+    ]
+    scores = [
+        lax.dot_general(
+            query[pl.ds(pl.multiple_of(sources[slot] * heads, heads), heads), :],
+            cache_ref[slot, :, :dim],
+            (((1,), (1,)), ((), ())),
+            preferred_element_type=F32,
+        )
+        for slot in range(slots)
+    ]
+    masked = [jnp.where(token < lives[slot], scores[slot] * scale, EMPTY) for slot in range(slots)]
+    maxima = [jnp.max(masked[slot], axis=1, keepdims=True) for slot in range(slots)]
     for slot in range(slots):
-        owner = owner_ref[slot]
-        used = owner >= 0
-        source = jnp.maximum(owner, 0)
-        live = jnp.where(used, length_ref[source] - block_ref[slot] * tokens, 0)
-        scores = (
-            lax.dot_general(
-                query[pl.ds(pl.multiple_of(source * heads, heads), heads), :],
-                cache_ref[slot, :, :dim],
-                (((1,), (1,)), ((), ())),
-                preferred_element_type=F32,
-            )
-            * scale
-        )
-        masked = jnp.where(token < live, scores, EMPTY)
-        block_max = jnp.max(masked, axis=1, keepdims=True)
-        weights = jnp.exp(masked - block_max)
-        block_sum = jnp.sum(weights, axis=1, keepdims=True)
-        block_out = jnp.dot(
-            weights.astype(BF16), cache_ref[slot, :, dim:], preferred_element_type=F32
-        )
-        places.append(pl.ds(pl.multiple_of(jnp.where(used, owner, requests) * heads, heads), heads))
-        maxima.append(jnp.broadcast_to(block_max, (heads, dim)))
-        sums.append(jnp.broadcast_to(block_sum, (heads, dim)))
-        outs.append(block_out)
-    for place, block_max in zip(places, maxima):
-        top[place, :] = jnp.maximum(top[place, :], block_max)
-    for place, block_max, block_sum, block_out in zip(places, maxima, sums, outs):
-        factor = jnp.exp(block_max - top[place, :])
-        total[place, :] = total[place, :] + factor * block_sum
-        summed[place, :] = summed[place, :] + factor * block_out
+        top[places[slot], :] = jnp.maximum(top[places[slot], :], maxima[slot])
+    weights = [jnp.exp(masked[slot] - maxima[slot]) for slot in range(slots)]
+    outs = [
+        jnp.dot(weights[slot].astype(BF16), cache_ref[slot, :, dim:], preferred_element_type=F32)
+        for slot in range(slots)
+    ]
+    sums = [jnp.sum(weights[slot], axis=1, keepdims=True) for slot in range(slots)]
+    factors = [jnp.exp(maxima[slot] - top[places[slot], :]) for slot in range(slots)]
+    for slot in range(slots):
+        place = places[slot]
+        total[place, :] = total[place, :] + factors[slot] * sums[slot]
+        summed[place, :] = summed[place, :] + factors[slot] * outs[slot]
     own_factor = jnp.exp(own_score - top[mine, :])
     total[mine, :] = total[mine, :] + own_factor
     summed[mine, :] = summed[mine, :] + own_factor * own_value
@@ -172,43 +176,13 @@
     return lax.ppermute(x, "req", [(place, place ^ distance) for place in range(size)])
 
 
-def on_device(
-    sizes, hidden, norm_gain, w_query, w_keyval, w_out, cache, slot_request, slot_block, cache_lengths
-):
-    requests = sizes["req"]
-    features = hidden.shape[1]
-    feature_rows = features // requests
-    query_weight = w_query.reshape(feature_rows, -1)
-    pair_weight = w_keyval.reshape(feature_rows, -1)
-    head_width = query_weight.shape[1]
-    lanes = pair_weight.shape[1]
+def attend(requests, mine, other, cache, slot_request, slot_block, cache_lengths):
+    slots, tokens, lanes = cache.shape
     dim = lanes // 2
-    heads = head_width // dim
+    heads = (mine.shape[1] - lanes) // dim
     rows = requests * heads
-    slots, tokens = cache.shape[1:3]
-
-    normed = call(
-        norm_kernel, (features // LANES, LANES), BF16, [VMEM, VMEM],
-        [pltpu.VMEM((features // LANES, LANES), F32)],
-    )(hidden, norm_gain.reshape(features // LANES, LANES))
-    columns = lax.all_to_all(
-        normed.reshape(requests, feature_rows // LANES, LANES), "req", 0, 0, tiled=True
-    )
-    sums = call(
-        project_kernel, (requests, head_width + lanes), F32, [VMEM] * 3, limit=16 * MIB,
-        flops=2 * requests * feature_rows * (head_width + lanes),
-        moved=2 * feature_rows * (head_width + lanes),
-    )(columns, query_weight, pair_weight)
-    distance = 1
-    while distance < requests:
-        other = exchanged(sums, distance, requests)
-        distance *= 2
-        if distance < requests:
-            sums = sums + other
-
-    me = lax.axis_index("req").astype(jnp.int32).reshape(1)
-    part = call(
-        attend_kernel, (dim + 8, rows), F32, [SMEM] * 4 + [VMEM] * 3,
+    return call(
+        attend_kernel, (dim + 8, rows), F32, [SMEM] * 3 + [VMEM] * 3,
         [
             pltpu.VMEM((rows, dim), F32),
             pltpu.VMEM((rows, dim), BF16),
@@ -221,13 +195,47 @@
         limit=16 * MIB,
         flops=2 * slots * tokens * heads * lanes,
         moved=2 * slots * tokens * lanes,
-    )(me, slot_request, slot_block, cache_lengths, sums, other, cache[0])
+    )(slot_request, slot_block, cache_lengths, mine, other, cache)
+
+
+def on_device(
+    sizes, hidden, norm_gain, w_query, w_keyval, w_out, cache, slot_request, slot_block, cache_lengths
+):
+    requests = sizes["req"]
+    features = hidden.shape[1]
+    feature_rows = features // requests
+    query_weight = w_query.reshape(feature_rows, -1)
+    pair_weight = w_keyval.reshape(feature_rows, -1)
+    head_width = query_weight.shape[1]
+    lanes = pair_weight.shape[1]
+    dim = lanes // 2
+    rows = requests * head_width // dim
+
+    shape = (features // LANES, LANES)
+    spread = call(spread_kernel, shape, F32, [VMEM])(hidden)
+    scaled = call(scale_kernel, shape, F32, [VMEM], flops=10**11)(spread)
+    columns = lax.all_to_all(
+        scaled.reshape(requests, feature_rows // LANES, LANES), "req", 0, 0, tiled=True
+    )
+    sums = call(
+        project_kernel, (requests, head_width + lanes), F32, [VMEM] * 4, limit=16 * MIB,
+        flops=2 * requests * feature_rows * (head_width + lanes),
+        moved=2 * feature_rows * (head_width + lanes),
+    )(columns, norm_gain.reshape(shape), query_weight, pair_weight)
+    distance = 1
+    while distance < requests:
+        other = exchanged(sums, distance, requests)
+        distance *= 2
+        if distance < requests:
+            sums = sums + other
+
+    part = attend(requests, sums, other, cache[0], slot_request, slot_block, cache_lengths)
     distance = 1
     while distance < requests:
         other = exchanged(part, distance, requests)
         distance *= 2
         if distance < requests:
-            part = call(merge_kernel, part.shape, F32, [VMEM] * 2)(part, other)
+            part = call(merge_kernel, part.shape, F32, [VMEM] * 2, moved=16 * MIB)(part, other)
 
     columns_out = w_out.shape[2]
     projected = call(

time: 76.9 us -> 61.1 us (0.79)
  local copies, waits for them, and re-layouts: 13.2 us -> 1.63 us
  Pallas kernels: 9.39 us -> 5.01 us
    unnamed x18 -> x22, local copies, waits for them, and re-layouts: 12.5 us -> 0.89 us
    pallas_call x5 -> x6, Pallas kernels: 8.1 us -> 3.71 us  [the longest x1 2.18 us: attend(): call(attend_kernel, (dim + 8, rows), F32, [SMEM] * 3 + [VMEM] * 3, [pltpu...]
where the time goes in v2:
time: 61.1 us; the launch traced here: 60.9 us
  waiting for transfers between devices  27.1 us (44%)
  blocking collectives  24.6 us (40%)
  Pallas kernels  5.01 us (8%)
  starting transfers between devices  2.27 us (4%)
  local copies, waits for them, and re-layouts  1.63 us (3%)
    ppermute x6, waiting for transfers between devices, exchanged(): lax.ppermute(x, 'req', [(place, place ^ distance) for place in range(size)])  27.1 us
    all_to_all x1, blocking collectives, on_device(): lax.all_to_all(scaled.reshape(requests, feature_rows // LANES, LANES), 'r...  14.2 us
    all_to_all x1, blocking collectives, on_device(): lax.all_to_all(projected.reshape(sizes['kv'] * requests, columns_out // L...  10.3 us
    ppermute x6, starting transfers between devices, exchanged(): lax.ppermute(x, 'req', [(place, place ^ distance) for place in range(size)])  2.27 us
    pallas_call x1, Pallas kernels, attend(): call(attend_kernel, (dim + 8, rows), F32, [SMEM] * 3 + [VMEM] * 3, [pltpu...  2.18 us
    pallas_call x1, Pallas kernels, on_device(): call(project_kernel, (requests, head_width + lanes), F32, [VMEM] * 4, lim...  1.34 us
    pallas_call x1, Pallas kernels, on_device(): call(output_kernel, (sizes['kv'], requests * columns_out // LANES, LANES)...  1.3 us
  transfers between devices with their start and end apart: 6, of which 6 were waited for; matrix products, arithmetic and copies ran while one was open for 0% of the time, Pallas kernels for 0%

profile of v2, /device:TPU:0, one launch (start us, length us, event | category | flops | bytes accessed | tf_op | source)
XLA Modules:
  0.0 60.9 jit_solution(8131399965114143563)
XLA Ops:
  0.0 0.0 copy-start.3
  0.0 0.8 %copy-done.3 = bf16[1,16384]{1,0:T(2,128)(2,1)S(1)} copy-done((bf16[1,16384]{1,0:T(2,128)(2,1)S(1)}, bf16[1,16384]{1,0:T(2,128)(2,1)}, u32[]{:S(2)}) %copy-start.3) | copy-done | bytes 32792
  0.8 0.0 slice-start.2
  0.9 0.0 copy-start
  0.9 0.0 copy-start.1
  0.9 0.0 copy-start.2
  0.9 0.0 slice-start.3
  0.9 0.1 shard_map.92
  1.1 0.0 copy-start.4
  1.1 0.0 copy-start.5
  1.1 0.0 copy-start.6
  1.1 14.2 %all_to_all.10.x_ref = f32[8,16,128]{2,1,0:T(8,128)S(1)} all-to-all(f32[8,16,128]{2,1,0:T(8,128)S(1)} %bitcast.17), channel_id=1, replica_groups=mesh['parts'=2,'kv'=2,'req'=8] {'req'}, dimensions={0} | all-to-all | bytes 131072 | tf_op jit(solution)/shard_map/all_to_all | solution.py:217
  15.3 0.0 slice-start
  15.3 0.0 copy-done
  15.3 0.0 copy-done.1
  15.3 0.0 copy-done.2
  15.3 0.0 slice-start.1
  15.4 1.3 %shard_map.93 = f32[8,2304]{1,0:T(8,128)S(1)} custom-call(f32[8,16,128]{2,1,0:T(8,128)S(1)} %all_to_all.10.x_ref, f32[128,128]{1,0:T(8,128)S(1)} %bitcast.16, bf16[2048,2048]{1,0:T(8,128)(2,1)S(1)} %bitcast.10, bf16[2048,256]{1,0:T(8,128)(2,1)S(1)} %bitcast.14), custom_call_target="tpu_custom_call" | custom-call | flops 75497472 | bytes 9437184 | tf_op jit(solution)/shard_map/pallas_call | solution.py:220
  16.7 0.4 collective-permute-start
  17.1 4.0 %collective-permute-done = f32[8,2304]{1,0:T(8,128)S(1)} collective-permute-done((f32[8,2304]{1,0:T(8,128)S(1)}, f32[8,2304]{1,0:T(8,128)S(1)}, u32[]{:S(2)}, u32[]{:S(2)}) %collective-permute-start) | collective-permute-done | bytes 73760 | tf_op jit(solution)/shard_map/ppermute | solution.py:176
  21.1 0.3 collective-permute-start.1
  21.3 4.5 %collective-permute-done.1 = f32[8,2304]{1,0:T(8,128)S(1)} collective-permute-done((f32[8,2304]{1,0:T(8,128)S(1)}, f32[8,2304]{1,0:T(8,128)S(1)}, u32[]{:S(2)}, u32[]{:S(2)}) %collective-permute-start.1) | collective-permute-done | bytes 73760 | tf_op jit(solution)/shard_map/ppermute | solution.py:176
  25.8 0.7 %collective-permute-start.2 = (f32[8,2304]{1,0:T(8,128)S(1)}, f32[8,2304]{1,0:T(8,128)S(1)}, u32[]{:S(2)}, u32[]{:S(2)}) collective-permute-start(f32[8,2304]{1,0:T(8,128)S(1)} %add.7.mine_ref), channel_id=1, source_target_pairs={{0,4},{1,5},{2,6},{3,7},{4,0},{5,1},{6,2},{7,3},{8,12},{9,13},{10,... | collective-permute-start | bytes 221192 | tf_op jit(solution)/shard_map/ppermute | solution.py:176
  26.5 5.4 %collective-permute-done.2.other_ref = f32[8,2304]{1,0:T(8,128)S(1)} collective-permute-done((f32[8,2304]{1,0:T(8,128)S(1)}, f32[8,2304]{1,0:T(8,128)S(1)}, u32[]{:S(2)}, u32[]{:S(2)}) %collective-permute-start.2) | collective-permute-done | bytes 73760 | tf_op jit(solution)/shard_map/ppermute | solution.py:176
  31.9 0.0 slice-done.2
  31.9 0.0 slice-done.3
  31.9 0.0 copy-done.4
  31.9 0.0 copy-done.5
  31.9 0.0 copy-done.6
  31.9 2.2 %shard_map.94.first_ref = f32[136,128]{1,0:T(8,128)S(1)} custom-call(s32[24]{0:T(128)S(1)} %copy-done.4, s32[24]{0:T(128)S(1)} %copy-done.5, s32[8]{0:T(128)S(1)} %copy-done.6, f32[8,2304]{1,0:T(8,128)S(1)} %add.7.mine_ref, f32[8,2304]{1,0:T(8,128)S(1)} %collective-permute-done.2.other_ref, bf16[24,512,256]{2,1,0:T(8,128)(2,1)S(1)} %bitcast.13), custom_call_target="tpu_custom_call" | custom-call | flops 100663296 | bytes 6291456 | tf_op jit(solution)/shard_map/pallas_call | solution.py:184
  34.1 0.7 %collective-permute-start.3 = (f32[136,128]{1,0:T(8,128)S(1)}, f32[136,128]{1,0:T(8,128)S(1)}, u32[]{:S(2)}, u32[]{:S(2)}) collective-permute-start(f32[136,128]{1,0:T(8,128)S(1)} %shard_map.94.first_ref), channel_id=1, source_target_pairs={{0,1},{1,0},{2,3},{3,2},{4,5},{5,4},{6,7},{7,6},{8,9},{9,8},{10,11... | collective-permute-start | bytes 208904 | tf_op jit(solution)/shard_map/ppermute | solution.py:176
  34.9 3.7 %collective-permute-done.3.second_ref = f32[136,128]{1,0:T(8,128)S(1)} collective-permute-done((f32[136,128]{1,0:T(8,128)S(1)}, f32[136,128]{1,0:T(8,128)S(1)}, u32[]{:S(2)}, u32[]{:S(2)}) %collective-permute-start.3) | collective-permute-done | bytes 69664 | tf_op jit(solution)/shard_map/ppermute | solution.py:176
  38.5 0.1 collective-permute-start.4
  38.6 4.3 %collective-permute-done.4.second_ref = f32[136,128]{1,0:T(8,128)S(1)} collective-permute-done((f32[136,128]{1,0:T(8,128)S(1)}, f32[136,128]{1,0:T(8,128)S(1)}, u32[]{:S(2)}, u32[]{:S(2)}) %collective-permute-start.4) | collective-permute-done | bytes 69664 | tf_op jit(solution)/shard_map/ppermute | solution.py:176
  42.9 0.1 collective-permute-start.5
  43.0 5.4 %collective-permute-done.5.second_ref = f32[136,128]{1,0:T(8,128)S(1)} collective-permute-done((f32[136,128]{1,0:T(8,128)S(1)}, f32[136,128]{1,0:T(8,128)S(1)}, u32[]{:S(2)}, u32[]{:S(2)}) %collective-permute-start.5) | collective-permute-done | bytes 69664 | tf_op jit(solution)/shard_map/ppermute | solution.py:176
  48.4 0.0 slice-done
  48.4 0.0 slice-done.1
  48.4 1.3 %shard_map.97 = f32[2,128,128]{2,1,0:T(8,128)S(1)} custom-call(f32[136,128]{1,0:T(8,128)S(1)} %shard_map.96.first_ref, f32[136,128]{1,0:T(8,128)S(1)} %collective-permute-done.5.second_ref, bf16[2048,2048]{1,0:T(8,128)(2,1)S(1)} %bitcast.9), custom_call_target="tpu_custom_call" | custom-call | flops 67108864 | bytes 8388608 | tf_op jit(solution)/shard_map/pallas_call | solution.py:241
  49.7 10.3 %all_to_all.11 = f32[16,16,128]{2,1,0:T(8,128)S(1)} all-to-all(f32[16,16,128]{2,1,0:T(8,128)S(1)} %bitcast.15), channel_id=1, replica_groups=mesh['parts'=2,'kv'=2,'req'=8] {'kv','req'}, dimensions={0} | all-to-all | bytes 262144 | tf_op jit(solution)/shard_map/all_to_all | solution.py:248
  60.0 0.1 reshape.32
  60.1 0.2 reduce_sum.9
  60.3 0.7 %convert_element_type.15 = bf16[1,16384]{1,0:T(2,128)(2,1)} reshape(bf16[16384]{0:T(1024)(128)(2,1)S(1)} %reduce_sum.9) | data formatting | bytes 65536 | tf_op jit(solution)/shard_map/convert_element_type | solution.py:253
  (7 shorter events, 0.1 us)
Async XLA Ops:
  0.0 0.8 %copy-start.3 = (bf16[1,16384]{1,0:T(2,128)(2,1)S(1)}, bf16[1,16384]{1,0:T(2,128)(2,1)}, u32[]{:S(2)}) copy-start(bf16[1,16384]{1,0:T(2,128)(2,1)} %hidden_ref.1) | copy-start | bytes 98308
  0.8 31.1 %slice-start.2 = ((s8[6291456]{0:T(1024)(128)(4,1)}), s8[4194304]{0:T(1024)(128)(4,1)S(1)}, s32[]{:S(2)}) async-start(s8[6291456]{0:T(1024)(128)(4,1)} %bitcast.11), calls=%async_computation.4 | async-start | bytes 8388608
  0.9 14.4 %copy-start = (bf16[2048,1,2048]{2,0,1:T(8,128)(2,1)S(1)}, bf16[2048,1,2048]{2,0,1:T(8,128)(2,1)}, u32[]{:S(2)}) copy-start(bf16[2048,1,2048]{2,0,1:T(8,128)(2,1)} %param.11) | copy-start | bytes 25165828
  0.9 14.4 %copy-start.1 = (bf16[2048,1,256]{2,0,1:T(8,128)(2,1)S(1)}, bf16[2048,1,256]{2,0,1:T(8,128)(2,1)}, u32[]{:S(2)}) copy-start(bf16[2048,1,256]{2,0,1:T(8,128)(2,1)} %param.12) | copy-start | bytes 3145732
  0.9 14.4 %copy-start.2 = (f32[16384]{0:T(1024)S(1)}, f32[16384]{0:T(1024)}, u32[]{:S(2)}) copy-start(f32[16384]{0:T(1024)} %param.10) | copy-start | bytes 196612
  0.9 31.0 %slice-start.3 = ((s8[6291456]{0:T(1024)(128)(4,1)}), s8[2097152]{0:T(1024)(128)(4,1)S(1)}, s32[]{:S(2)}) async-start(s8[6291456]{0:T(1024)(128)(4,1)} %bitcast.11), calls=%async_computation.5 | async-start | bytes 4194304
  1.1 30.9 %copy-start.4 = (s32[24]{0:T(128)S(1)}, s32[24]{0:T(128)}, u32[]{:S(2)}) copy-start(s32[24]{0:T(128)} %owner_ref.1) | copy-start | bytes 292
  1.1 30.9 %copy-start.5 = (s32[24]{0:T(128)S(1)}, s32[24]{0:T(128)}, u32[]{:S(2)}) copy-start(s32[24]{0:T(128)} %block_ref.1) | copy-start | bytes 292
  1.1 30.9 %copy-start.6 = (s32[8]{0:T(128)S(1)}, s32[8]{0:T(128)}, u32[]{:S(2)}) copy-start(s32[8]{0:T(128)} %length_ref.1) | copy-start | bytes 100
  15.3 33.1 %slice-start = ((s8[8388608]{0:T(1024)(128)(4,1)}), s8[4194304]{0:T(1024)(128)(4,1)S(1)}, s32[]{:S(2)}) async-start(s8[8388608]{0:T(1024)(128)(4,1)} %bitcast.7), calls=%async_computation.2 | async-start | bytes 8388608
  15.3 33.1 %slice-start.1 = ((s8[8388608]{0:T(1024)(128)(4,1)}), s8[4194304]{0:T(1024)(128)(4,1)S(1)}, s32[]{:S(2)}) async-start(s8[8388608]{0:T(1024)(128)(4,1)} %bitcast.7), calls=%async_computation.3 | async-start | bytes 8388608
  16.7 4.4 %collective-permute-start = (f32[8,2304]{1,0:T(8,128)S(1)}, f32[8,2304]{1,0:T(8,128)S(1)}, u32[]{:S(2)}, u32[]{:S(2)}) collective-permute-start(f32[8,2304]{1,0:T(8,128)S(1)} %shard_map.93), channel_id=1, source_target_pairs={{0,1},{1,0},{2,3},{3,2},{4,5},{5,4},{6,7},{7,6},{8,9},{9,8},{10,11... | collective-permute-start | bytes 221192 | tf_op jit(solution)/shard_map/ppermute | solution.py:176
  21.1 4.7 %collective-permute-start.1 = (f32[8,2304]{1,0:T(8,128)S(1)}, f32[8,2304]{1,0:T(8,128)S(1)}, u32[]{:S(2)}, u32[]{:S(2)}) collective-permute-start(f32[8,2304]{1,0:T(8,128)S(1)} %add.6), channel_id=1, source_target_pairs={{0,2},{1,3},{2,0},{3,1},{4,6},{5,7},{6,4},{7,5},{8,10},{9,11},{10,... | collective-permute-start | bytes 221192 | tf_op jit(solution)/shard_map/ppermute | solution.py:176
  25.8 6.1 %collective-permute-start.2 = (f32[8,2304]{1,0:T(8,128)S(1)}, f32[8,2304]{1,0:T(8,128)S(1)}, u32[]{:S(2)}, u32[]{:S(2)}) collective-permute-start(f32[8,2304]{1,0:T(8,128)S(1)} %add.7.mine_ref), channel_id=1, source_target_pairs={{0,4},{1,5},{2,6},{3,7},{4,0},{5,1},{6,2},{7,3},{8,12},{9,13},{10,... | collective-permute-start | bytes 221192 | tf_op jit(solution)/shard_map/ppermute | solution.py:176
  34.1 4.4 %collective-permute-start.3 = (f32[136,128]{1,0:T(8,128)S(1)}, f32[136,128]{1,0:T(8,128)S(1)}, u32[]{:S(2)}, u32[]{:S(2)}) collective-permute-start(f32[136,128]{1,0:T(8,128)S(1)} %shard_map.94.first_ref), channel_id=1, source_target_pairs={{0,1},{1,0},{2,3},{3,2},{4,5},{5,4},{6,7},{7,6},{8,9},{9,8},{10,11... | collective-permute-start | bytes 208904 | tf_op jit(solution)/shard_map/ppermute | solution.py:176
  38.5 4.4 %collective-permute-start.4 = (f32[136,128]{1,0:T(8,128)S(1)}, f32[136,128]{1,0:T(8,128)S(1)}, u32[]{:S(2)}, u32[]{:S(2)}) collective-permute-start(f32[136,128]{1,0:T(8,128)S(1)} %shard_map.95.first_ref), channel_id=1, source_target_pairs={{0,2},{1,3},{2,0},{3,1},{4,6},{5,7},{6,4},{7,5},{8,10},{9,11},{10,... | collective-permute-start | bytes 208904 | tf_op jit(solution)/shard_map/ppermute | solution.py:176
  42.9 5.5 %collective-permute-start.5 = (f32[136,128]{1,0:T(8,128)S(1)}, f32[136,128]{1,0:T(8,128)S(1)}, u32[]{:S(2)}, u32[]{:S(2)}) collective-permute-start(f32[136,128]{1,0:T(8,128)S(1)} %shard_map.96.first_ref), channel_id=1, source_target_pairs={{0,4},{1,5},{2,6},{3,7},{4,0},{5,1},{6,2},{7,3},{8,12},{9,13},{10,... | collective-permute-start | bytes 208904 | tf_op jit(solution)/shard_map/ppermute | solution.py:176

commit v3 on v2

--- a/solution.py
+++ b/solution.py
@@ -42,23 +42,36 @@
     out_ref[:, width:] = jnp.dot(x, pair_ref[...], preferred_element_type=F32)
 
 
+def spread_sum_kernel(first_ref, second_ref, out_ref):
+    total = first_ref[...] + second_ref[...]
+    for copy in range(out_ref.shape[0]):
+        out_ref[copy, :, :] = total
+
+
 def attend_kernel(
-    owner_ref, block_ref, length_ref, mine_ref, other_ref, cache_ref, out_ref,
+    owner_ref, block_ref, length_ref, parts_ref, cache_ref, out_ref,
     wide, query, new_key, new_value, top, total, summed,
 ):
-    requests = mine_ref.shape[0]
+    near, requests, width = parts_ref.shape
     slots, tokens, lanes = cache_ref.shape
     dim = lanes // 2
-    heads = (mine_ref.shape[1] - lanes) // dim
+    heads = (width - lanes) // dim
+
+    def summed_parts(at):
+        so_far = parts_ref[0, :, at]
+        for index in range(1, near):
+            so_far = so_far + parts_ref[index, :, at]
+        return so_far
+
     scale = dim ** (-0.5)
     rows = requests * heads
     for head in range(heads):
         at = slice(head * dim, (head + 1) * dim)
-        wide[pl.ds(head, requests, stride=heads), :] = mine_ref[:, at] + other_ref[:, at]
+        wide[pl.ds(head, requests, stride=heads), :] = summed_parts(at)
     query[...] = wide[...].astype(BF16)
     for new, start in ((new_key, heads * dim), (new_value, heads * dim + dim)):
         at = slice(start, start + dim)
-        new[...] = (mine_ref[:, at] + other_ref[:, at]).astype(BF16).astype(F32)
+        new[...] = summed_parts(at).astype(BF16).astype(F32)
 
     me = lax.axis_index("req").astype(jnp.int32)
     mine = pl.ds(pl.multiple_of(me * heads, heads), heads)
@@ -117,32 +130,35 @@
     out_ref[dim + 2 :, :] = jnp.zeros((out_ref.shape[0] - dim - 2, rows), F32)
 
 
-def merged(first_ref, second_ref):
+def merged(parts):
     dim = LANES
-    first_top = first_ref[dim : dim + 1, :]
-    second_top = second_ref[dim : dim + 1, :]
-    top = jnp.maximum(first_top, second_top)
-    first_factor = jnp.exp(first_top - top)
-    second_factor = jnp.exp(second_top - top)
-    total = (
-        first_ref[dim + 1 : dim + 2, :] * first_factor
-        + second_ref[dim + 1 : dim + 2, :] * second_factor
-    )
-    summed = first_ref[:dim, :] * first_factor + second_ref[:dim, :] * second_factor
+    tops = [part[dim : dim + 1, :] for part in parts]
+    top = tops[0]
+    for other in tops[1:]:
+        top = jnp.maximum(top, other)
+    total = None
+    summed = None
+    for part, part_top in zip(parts, tops):
+        factor = jnp.exp(part_top - top)
+        part_total = part[dim + 1 : dim + 2, :] * factor
+        part_summed = part[:dim, :] * factor
+        total = part_total if total is None else total + part_total
+        summed = part_summed if summed is None else summed + part_summed
     return top, total, summed
 
 
 def merge_kernel(first_ref, second_ref, out_ref):
     dim = LANES
-    top, total, summed = merged(first_ref, second_ref)
-    out_ref[:dim, :] = summed
-    out_ref[dim : dim + 1, :] = top
-    out_ref[dim + 1 : dim + 2, :] = total
-    out_ref[dim + 2 :, :] = jnp.zeros((out_ref.shape[0] - dim - 2, out_ref.shape[1]), F32)
-
-
-def output_kernel(first_ref, second_ref, weight_ref, out_ref, rows):
-    _, total, summed = merged(first_ref, second_ref)
+    top, total, summed = merged([first_ref, second_ref])
+    for copy in range(out_ref.shape[0]):
+        out_ref[copy, :dim, :] = summed
+        out_ref[copy, dim : dim + 1, :] = top
+        out_ref[copy, dim + 1 : dim + 2, :] = total
+        out_ref[copy, dim + 2 :, :] = jnp.zeros((out_ref.shape[1] - dim - 2, out_ref.shape[2]), F32)
+
+
+def output_kernel(parts_ref, weight_ref, out_ref, rows):
+    _, total, summed = merged([parts_ref.at[index] for index in range(parts_ref.shape[0])])
     rows[...] = (summed / total).T
     heads = weight_ref.shape[0] // LANES
     requests = rows.shape[0] // heads
@@ -156,8 +172,11 @@
         y = jnp.dot(x, weight_ref[:, at : at + step], preferred_element_type=F32)
         for chunk in range(step // LANES):
             part = y[:, chunk * LANES : (chunk + 1) * LANES]
-            for copy in range(out_ref.shape[0]):
-                out_ref[copy, pl.ds(at // LANES + chunk, requests, stride=chunks), :] = part
+            out_ref[pl.ds(at // LANES + chunk, requests, stride=chunks), :] = part
+
+
+def round_sum_kernel(first_ref, second_ref, out_ref):
+    out_ref[...] = (first_ref[...] + second_ref[...]).astype(BF16)
 
 
 def call(kernel, shape, dtype, in_specs, scratch=(), limit=4 * MIB, flops=0, moved=0):
@@ -176,13 +195,13 @@
     return lax.ppermute(x, "req", [(place, place ^ distance) for place in range(size)])
 
 
-def attend(requests, mine, other, cache, slot_request, slot_block, cache_lengths):
+def attend(requests, parts, cache, slot_request, slot_block, cache_lengths):
     slots, tokens, lanes = cache.shape
     dim = lanes // 2
-    heads = (mine.shape[1] - lanes) // dim
+    heads = (parts.shape[2] - lanes) // dim
     rows = requests * heads
     return call(
-        attend_kernel, (dim + 8, rows), F32, [SMEM] * 3 + [VMEM] * 3,
+        attend_kernel, (dim + 8, rows), F32, [SMEM] * 3 + [VMEM] * 2,
         [
             pltpu.VMEM((rows, dim), F32),
             pltpu.VMEM((rows, dim), BF16),
@@ -195,7 +214,7 @@
         limit=16 * MIB,
         flops=2 * slots * tokens * heads * lanes,
         moved=2 * slots * tokens * lanes,
-    )(slot_request, slot_block, cache_lengths, mine, other, cache)
+    )(slot_request, slot_block, cache_lengths, parts, cache)
 
 
 def on_device(
@@ -222,35 +241,42 @@
         flops=2 * requests * feature_rows * (head_width + lanes),
         moved=2 * feature_rows * (head_width + lanes),
     )(columns, norm_gain.reshape(shape), query_weight, pair_weight)
-    distance = 1
-    while distance < requests:
-        other = exchanged(sums, distance, requests)
-        distance *= 2
-        if distance < requests:
-            sums = sums + other
-
-    part = attend(requests, sums, other, cache[0], slot_request, slot_block, cache_lengths)
-    distance = 1
-    while distance < requests:
-        other = exchanged(part, distance, requests)
-        distance *= 2
-        if distance < requests:
-            part = call(merge_kernel, part.shape, F32, [VMEM] * 2, moved=16 * MIB)(part, other)
+    near = min(4, requests)
+    groups = [list(range(at, at + near)) for at in range(0, requests, near)]
+
+    def far_then_near(x, combine, combine_and_copy):
+        distance = requests // 2
+        while distance > near:
+            x = combine(x, exchanged(x, distance, requests))
+            distance //= 2
+        x = combine_and_copy(x, exchanged(x, distance, requests))
+        return lax.all_to_all(x, "req", 0, 0, tiled=True, axis_index_groups=groups)
+
+    sums = far_then_near(
+        sums, lambda x, y: x + y,
+        lambda x, y: call(spread_sum_kernel, (near,) + x.shape, F32, [VMEM] * 2)(x, y),
+    )
+    part = attend(requests, sums, cache[0], slot_request, slot_block, cache_lengths)
+
+    def merge(x, y, copies):
+        return call(merge_kernel, (copies,) + x.shape, F32, [VMEM] * 2, moved=16 * MIB)(x, y)
+
+    parts = far_then_near(part, lambda x, y: merge(x, y, 1)[0], lambda x, y: merge(x, y, near))
 
     columns_out = w_out.shape[2]
     projected = call(
-        output_kernel, (sizes["kv"], requests * columns_out // LANES, LANES), F32, [VMEM] * 3,
+        output_kernel, (requests * columns_out // LANES, LANES), F32, [VMEM] * 2,
         [pltpu.VMEM((rows, dim), F32)],
         limit=16 * MIB,
         flops=2 * requests * head_width * columns_out,
         moved=2 * head_width * columns_out,
-    )(part, other, w_out[0])
-    terms = lax.all_to_all(
-        projected.reshape(sizes["kv"] * requests, columns_out // LANES, LANES),
-        ("kv", "req"), 0, 0, tiled=True,
-    )
-    terms = terms.reshape(sizes["kv"], -1)
-    return jnp.sum(terms, axis=0, keepdims=True).astype(BF16)
+    )(parts, w_out[0])
+    other = lax.ppermute(projected, "kv", [(0, 1), (1, 0)])
+    total = call(round_sum_kernel, projected.shape, BF16, [VMEM] * 2)(projected, other)
+    result = lax.all_to_all(
+        total.reshape(requests, columns_out // LANES, LANES), "req", 0, 0, tiled=True
+    )
+    return result.reshape(1, -1)
 
 
 def solution(mesh):

time: 61.1 us -> 60.3 us (0.987)
  blocking collectives: 24.6 us -> 40.3 us
  waiting for transfers between devices: 27.1 us -> 12 us
  starting transfers between devices: 2.27 us -> 0.99 us
    ppermute x6 -> x2, waiting for transfers between devices: 27.1 us -> 10.7 us  [exchanged(): lax.ppermute(x, 'req', [(place, place ^ distance) for place in range(size)])]
    all_to_all x1 -> x3, blocking collectives: 10.3 us -> 26.1 us  [the longest x2 17 us: far_then_near(): return lax.all_to_all(x, 'req', 0, 0, tiled=True, axis_index_groups=groups)]
    ppermute x6 -> x2, starting transfers between devices: 2.27 us -> 0.99 us  [exchanged(): lax.ppermute(x, 'req', [(place, place ^ distance) for place in range(size)])]
    ppermute x0 -> x1, waiting for transfers between devices: none -> 1.25 us  [on_device(): other = lax.ppermute(projected, 'kv', [(0, 1), (1, 0)])]
    convert_element_type x1 -> x0, local copies, waits for them, and re-layouts: 0.67 us -> none  [on_device(): return jnp.sum(terms, axis=0, keepdims=True).astype(BF16)]
    pallas_call x4 -> x5, Pallas kernels: 3.51 us -> 3.54 us  [the longest x1 2.18 us: attend(): call(attend_kernel, (dim + 8, rows), F32, [SMEM] * 3 + [VMEM] * 2, [pltpu...]
  transfers between devices with their start and end apart: 6 -> 3, of which waited for: 6 -> 3; matrix products, arithmetic and copies ran while one was open for 0% -> 0% of each run, Pallas kernels for 0% -> 0%
where the time goes in v3:
time: 60.3 us; the launch traced here: 60 us
  blocking collectives  40.3 us (67%)
  waiting for transfers between devices  12 us (20%)
  Pallas kernels  5.03 us (8%)
  local copies, waits for them, and re-layouts  1.54 us (3%)
  starting transfers between devices  0.99 us (2%)
    all_to_all x2, blocking collectives, far_then_near(): return lax.all_to_all(x, 'req', 0, 0, tiled=True, axis_index_groups=groups)  17 us
    all_to_all x1, blocking collectives, on_device(): lax.all_to_all(scaled.reshape(requests, feature_rows // LANES, LANES), 'r...  14.2 us
    ppermute x2, waiting for transfers between devices, exchanged(): lax.ppermute(x, 'req', [(place, place ^ distance) for place in range(size)])  10.7 us
    all_to_all x1, blocking collectives, on_device(): lax.all_to_all(total.reshape(requests, columns_out // LANES, LANES), 'req...  9.06 us
    pallas_call x1, Pallas kernels, attend(): call(attend_kernel, (dim + 8, rows), F32, [SMEM] * 3 + [VMEM] * 2, [pltpu...  2.18 us
    pallas_call x1, Pallas kernels, on_device(): call(project_kernel, (requests, head_width + lanes), F32, [VMEM] * 4, lim...  1.34 us
    pallas_call x1, Pallas kernels, on_device(): call(output_kernel, (requests * columns_out // LANES, LANES), F32, [VMEM]...  1.29 us
    ppermute x1, waiting for transfers between devices, on_device(): other = lax.ppermute(projected, 'kv', [(0, 1), (1, 0)])  1.25 us
  transfers between devices with their start and end apart: 3, of which 3 were waited for; matrix products, arithmetic and copies ran while one was open for 0% of the time, Pallas kernels for 0%

profile of v3, /device:TPU:0, one launch (start us, length us, event | category | flops | bytes accessed | tf_op | source)
XLA Modules:
  0.0 60.0 jit_solution(3278081361644450028)
XLA Ops:
  0.0 0.0 copy-start.3
  0.0 0.8 %copy-done.3 = bf16[1,16384]{1,0:T(2,128)(2,1)S(1)} copy-done((bf16[1,16384]{1,0:T(2,128)(2,1)S(1)}, bf16[1,16384]{1,0:T(2,128)(2,1)}, u32[]{:S(2)}) %copy-start.3) | copy-done | bytes 32792
  0.8 0.0 slice-start.2
  0.9 0.0 copy-start
  0.9 0.0 copy-start.1
  0.9 0.0 copy-start.2
  0.9 0.0 slice-start.3
  0.9 0.1 shard_map.92
  1.1 0.0 copy-start.4
  1.1 0.0 copy-start.5
  1.1 0.0 copy-start.6
  1.1 14.2 %all_to_all.20.x_ref = f32[8,16,128]{2,1,0:T(8,128)S(1)} all-to-all(f32[8,16,128]{2,1,0:T(8,128)S(1)} %bitcast.17), channel_id=1, replica_groups=mesh['parts'=2,'kv'=2,'req'=8] {'req'}, dimensions={0} | all-to-all | bytes 131072 | tf_op jit(solution)/shard_map/all_to_all | solution.py:236
  15.3 0.0 slice-start
  15.3 0.0 copy-done
  15.3 0.0 copy-done.1
  15.3 0.0 copy-done.2
  15.3 0.0 slice-start.1
  15.4 1.3 %shard_map.93.first_ref = f32[8,2304]{1,0:T(8,128)S(1)} custom-call(f32[8,16,128]{2,1,0:T(8,128)S(1)} %all_to_all.20.x_ref, f32[128,128]{1,0:T(8,128)S(1)} %bitcast.16, bf16[2048,2048]{1,0:T(8,128)(2,1)S(1)} %bitcast.7, bf16[2048,256]{1,0:T(8,128)(2,1)S(1)} %bitcast.14), custom_call_target="tpu_custom_call" | custom-call | flops 75497472 | bytes 9437184 | tf_op jit(solution)/shard_map/pallas_call | solution.py:239
  16.7 0.5 collective-permute-start
  17.2 5.2 %collective-permute-done.second_ref = f32[8,2304]{1,0:T(8,128)S(1)} collective-permute-done((f32[8,2304]{1,0:T(8,128)S(1)}, f32[8,2304]{1,0:T(8,128)S(1)}, u32[]{:S(2)}, u32[]{:S(2)}) %collective-permute-start) | collective-permute-done | bytes 73760 | tf_op jit(solution)/shard_map/ppermute | solution.py:195
  22.4 8.5 %all_to_all.21.parts_ref = f32[4,8,2304]{2,1,0:T(8,128)S(1)} all-to-all(f32[4,8,2304]{2,1,0:T(8,128)S(1)} %shard_map.94), channel_id=1, replica_groups={{0,1,2,3},{4,5,6,7},{8,9,10,11},{12,13,14,15},{16,17,18,19},{20,21,22,2..., dimensions={0} | all-to-all | bytes 589824 | tf_op jit(solution)/shard_map/all_to_all | solution.py:253
  30.9 0.0 slice-done.2
  30.9 0.0 slice-done.3
  30.9 0.0 copy-done.4
  30.9 0.0 copy-done.5
  31.0 0.0 copy-done.6
  31.0 2.2 %shard_map.95.first_ref = f32[136,128]{1,0:T(8,128)S(1)} custom-call(s32[24]{0:T(128)S(1)} %copy-done.4, s32[24]{0:T(128)S(1)} %copy-done.5, s32[8]{0:T(128)S(1)} %copy-done.6, f32[4,8,2304]{2,1,0:T(8,128)S(1)} %all_to_all.21.parts_ref, bf16[24,512,256]{2,1,0:T(8,128)(2,1)S(1)} %bitcast.13), custom_call_target="tpu_custom_call" | custom-call | flops 100663296 | bytes 6291456 | tf_op jit(solution)/shard_map/pallas_call | solution.py:203
  33.2 0.5 collective-permute-start.1
  33.7 5.5 %collective-permute-done.1.second_ref = f32[136,128]{1,0:T(8,128)S(1)} collective-permute-done((f32[136,128]{1,0:T(8,128)S(1)}, f32[136,128]{1,0:T(8,128)S(1)}, u32[]{:S(2)}, u32[]{:S(2)}) %collective-permute-start.1) | collective-permute-done | bytes 69664 | tf_op jit(solution)/shard_map/ppermute | solution.py:195
  39.2 8.5 %all_to_all.22.parts_ref = f32[4,136,128]{2,1,0:T(8,128)S(1)} all-to-all(f32[4,136,128]{2,1,0:T(8,128)S(1)} %shard_map.96), channel_id=1, replica_groups={{0,1,2,3},{4,5,6,7},{8,9,10,11},{12,13,14,15},{16,17,18,19},{20,21,22,2..., dimensions={0} | all-to-all | bytes 557056 | tf_op jit(solution)/shard_map/all_to_all | solution.py:253
  47.7 0.0 slice-done
  47.7 0.0 slice-done.1
  47.7 1.3 %shard_map.97.first_ref = f32[128,128]{1,0:T(8,128)S(1)} custom-call(f32[4,136,128]{2,1,0:T(8,128)S(1)} %all_to_all.22.parts_ref, bf16[2048,2048]{1,0:T(8,128)(2,1)S(1)} %bitcast.10), custom_call_target="tpu_custom_call" | custom-call | flops 67108864 | bytes 8388608 | tf_op jit(solution)/shard_map/pallas_call | solution.py:267
  49.0 0.0 collective-permute-start.2
  49.0 1.2 %collective-permute-done.2.second_ref = f32[128,128]{1,0:T(8,128)S(1)} collective-permute-done((f32[128,128]{1,0:T(8,128)S(1)}, f32[128,128]{1,0:T(8,128)S(1)}, u32[]{:S(2)}, u32[]{:S(2)}) %collective-permute-start.2) | collective-permute-done | bytes 65568 | tf_op jit(solution)/shard_map/ppermute | solution.py:274
  50.3 9.1 %all_to_all.23 = bf16[8,16,128]{2,1,0:T(8,128)(2,1)S(1)} all-to-all(bf16[8,16,128]{2,1,0:T(8,128)(2,1)S(1)} %bitcast.15), channel_id=1, replica_groups=mesh['parts'=2,'kv'=2,'req'=8] {'req'}, dimensions={0} | all-to-all | bytes 65536 | tf_op jit(solution)/shard_map/all_to_all | solution.py:276
  59.3 0.6 %reshape.23 = bf16[1,16384]{1,0:T(2,128)(2,1)} reshape(bf16[8,16,128]{2,1,0:T(8,128)(2,1)S(1)} %all_to_all.23) | data formatting | bytes 65536 | tf_op jit(solution)/shard_map/reshape | solution.py:279
  (6 shorter events, 0.1 us)
Async XLA Ops:
  0.0 0.8 %copy-start.3 = (bf16[1,16384]{1,0:T(2,128)(2,1)S(1)}, bf16[1,16384]{1,0:T(2,128)(2,1)}, u32[]{:S(2)}) copy-start(bf16[1,16384]{1,0:T(2,128)(2,1)} %hidden_ref.1) | copy-start | bytes 98308
  0.8 30.1 %slice-start.2 = ((s8[6291456]{0:T(1024)(128)(4,1)}), s8[4194304]{0:T(1024)(128)(4,1)S(1)}, s32[]{:S(2)}) async-start(s8[6291456]{0:T(1024)(128)(4,1)} %bitcast.11), calls=%async_computation.6 | async-start | bytes 8388608
  0.9 14.4 %copy-start = (bf16[2048,1,2048]{2,0,1:T(8,128)(2,1)S(1)}, bf16[2048,1,2048]{2,0,1:T(8,128)(2,1)}, u32[]{:S(2)}) copy-start(bf16[2048,1,2048]{2,0,1:T(8,128)(2,1)} %param.11) | copy-start | bytes 25165828
  0.9 14.4 %copy-start.1 = (bf16[2048,1,256]{2,0,1:T(8,128)(2,1)S(1)}, bf16[2048,1,256]{2,0,1:T(8,128)(2,1)}, u32[]{:S(2)}) copy-start(bf16[2048,1,256]{2,0,1:T(8,128)(2,1)} %param.12) | copy-start | bytes 3145732
  0.9 14.4 %copy-start.2 = (f32[16384]{0:T(1024)S(1)}, f32[16384]{0:T(1024)}, u32[]{:S(2)}) copy-start(f32[16384]{0:T(1024)} %param.10) | copy-start | bytes 196612
  0.9 30.0 %slice-start.3 = ((s8[6291456]{0:T(1024)(128)(4,1)}), s8[2097152]{0:T(1024)(128)(4,1)S(1)}, s32[]{:S(2)}) async-start(s8[6291456]{0:T(1024)(128)(4,1)} %bitcast.11), calls=%async_computation.7 | async-start | bytes 4194304
  1.1 29.9 %copy-start.4 = (s32[24]{0:T(128)S(1)}, s32[24]{0:T(128)}, u32[]{:S(2)}) copy-start(s32[24]{0:T(128)} %owner_ref.1) | copy-start | bytes 292
  1.1 29.9 %copy-start.5 = (s32[24]{0:T(128)S(1)}, s32[24]{0:T(128)}, u32[]{:S(2)}) copy-start(s32[24]{0:T(128)} %block_ref.1) | copy-start | bytes 292
  1.1 29.9 %copy-start.6 = (s32[8]{0:T(128)S(1)}, s32[8]{0:T(128)}, u32[]{:S(2)}) copy-start(s32[8]{0:T(128)} %length_ref.1) | copy-start | bytes 100
  15.3 32.4 %slice-start = ((s8[8388608]{0:T(1024)(128)(4,1)}), s8[4194304]{0:T(1024)(128)(4,1)S(1)}, s32[]{:S(2)}) async-start(s8[8388608]{0:T(1024)(128)(4,1)} %bitcast.8), calls=%async_computation.4 | async-start | bytes 8388608
  15.3 32.4 %slice-start.1 = ((s8[8388608]{0:T(1024)(128)(4,1)}), s8[4194304]{0:T(1024)(128)(4,1)S(1)}, s32[]{:S(2)}) async-start(s8[8388608]{0:T(1024)(128)(4,1)} %bitcast.8), calls=%async_computation.5 | async-start | bytes 8388608
  16.7 5.7 %collective-permute-start = (f32[8,2304]{1,0:T(8,128)S(1)}, f32[8,2304]{1,0:T(8,128)S(1)}, u32[]{:S(2)}, u32[]{:S(2)}) collective-permute-start(f32[8,2304]{1,0:T(8,128)S(1)} %shard_map.93.first_ref), channel_id=1, source_target_pairs={{0,4},{1,5},{2,6},{3,7},{4,0},{5,1},{6,2},{7,3},{8,12},{9,13},{10,... | collective-permute-start | bytes 221192 | tf_op jit(solution)/shard_map/ppermute | solution.py:195
  33.2 6.0 %collective-permute-start.1 = (f32[136,128]{1,0:T(8,128)S(1)}, f32[136,128]{1,0:T(8,128)S(1)}, u32[]{:S(2)}, u32[]{:S(2)}) collective-permute-start(f32[136,128]{1,0:T(8,128)S(1)} %shard_map.95.first_ref), channel_id=1, source_target_pairs={{0,4},{1,5},{2,6},{3,7},{4,0},{5,1},{6,2},{7,3},{8,12},{9,13},{10,... | collective-permute-start | bytes 208904 | tf_op jit(solution)/shard_map/ppermute | solution.py:195
  49.0 1.3 %collective-permute-start.2 = (f32[128,128]{1,0:T(8,128)S(1)}, f32[128,128]{1,0:T(8,128)S(1)}, u32[]{:S(2)}, u32[]{:S(2)}) collective-permute-start(f32[128,128]{1,0:T(8,128)S(1)} %shard_map.97.first_ref), channel_id=1, source_target_pairs={{0,8},{8,0},{1,9},{9,1},{2,10},{10,2},{3,11},{11,3},{4,12},{12,4},... | collective-permute-start | bytes 196616 | tf_op jit(solution)/shard_map/ppermute | solution.py:274

commit v4 on v3

--- a/solution.py
+++ b/solution.py
@@ -36,32 +36,59 @@
     width = query_ref.shape[1]
     step = 512
     for at in range(0, width, step):
-        out_ref[:, at : at + step] = jnp.dot(
-            x, query_ref[:, at : at + step], preferred_element_type=F32
+        y = jnp.dot(x, query_ref[:, at : at + step], preferred_element_type=F32)
+        for copy in range(out_ref.shape[0]):
+            out_ref[copy, :, at : at + step] = y
+    y = jnp.dot(x, pair_ref[...], preferred_element_type=F32)
+    for copy in range(out_ref.shape[0]):
+        out_ref[copy, :, width:] = y
+
+
+def sum_kernel(parts_ref, out_ref):
+    total = parts_ref[0]
+    for index in range(1, parts_ref.shape[0]):
+        total = total + parts_ref[index]
+    out_ref[...] = total
+
+
+def slots_kernel(owner_ref, block_ref, length_ref, place_ref, pick_ref, live_ref, tokens):
+    slots = owner_ref.shape[0]
+    requests = length_ref.shape[0]
+    lane = lax.broadcasted_iota(jnp.int32, place_ref.shape, 1)
+    places = jnp.zeros(place_ref.shape, jnp.int32)
+    heads = pick_ref.shape[0] // slots
+    shape = (heads, pick_ref.shape[1])
+    offset = lax.broadcasted_iota(jnp.int32, shape, 1) - lax.broadcasted_iota(jnp.int32, shape, 0)
+    for slot in range(slots):
+        owner = owner_ref[slot]
+        live = jnp.where(
+            owner >= 0, length_ref[jnp.maximum(owner, 0)] - block_ref[slot] * tokens, 0
         )
-    out_ref[:, width:] = jnp.dot(x, pair_ref[...], preferred_element_type=F32)
-
-
-def spread_sum_kernel(first_ref, second_ref, out_ref):
-    total = first_ref[...] + second_ref[...]
-    for copy in range(out_ref.shape[0]):
-        out_ref[copy, :, :] = total
+        place = jnp.where(owner >= 0, owner, requests) * heads
+        places = jnp.where(lane == slot, place, places)
+        rows = slice(slot * heads, (slot + 1) * heads)
+        pick_ref[rows, :] = jnp.where(offset == owner * heads, 1.0, 0.0).astype(BF16)
+        live_ref[rows, :] = jnp.full((heads, LANES), live, jnp.int32)
+    place_ref[...] = places
+
+
+def keys_kernel(cache_ref, out_ref):
+    dim = out_ref.shape[1]
+    for slot in range(cache_ref.shape[0]):
+        out_ref[slot, :, :] = cache_ref[slot, :, :dim].T
 
 
 def attend_kernel(
-    owner_ref, block_ref, length_ref, parts_ref, cache_ref, out_ref,
+    place_ref, pick_ref, live_ref, first_ref, second_ref, key_ref, cache_ref, out_ref,
     wide, query, new_key, new_value, top, total, summed,
 ):
-    near, requests, width = parts_ref.shape
+    requests, width = first_ref.shape
     slots, tokens, lanes = cache_ref.shape
     dim = lanes // 2
     heads = (width - lanes) // dim
 
     def summed_parts(at):
-        so_far = parts_ref[0, :, at]
-        for index in range(1, near):
-            so_far = so_far + parts_ref[index, :, at]
-        return so_far
+        return first_ref[:, at] + second_ref[:, at]
 
     scale = dim ** (-0.5)
     rows = requests * heads
@@ -85,28 +112,24 @@
     summed[...] = jnp.zeros(summed.shape, F32)
     top[mine, :] = jnp.broadcast_to(own_score, (heads, dim))
 
-    token = lax.broadcasted_iota(jnp.int32, (heads, tokens), 1)
-    owners = [owner_ref[slot] for slot in range(slots)]
-    sources = [jnp.maximum(owner, 0) for owner in owners]
-    lives = [
-        jnp.where(owners[slot] >= 0, length_ref[sources[slot]] - block_ref[slot] * tokens, 0)
-        for slot in range(slots)
-    ]
-    places = [
-        pl.ds(pl.multiple_of(jnp.where(owner >= 0, owner, requests) * heads, heads), heads)
-        for owner in owners
-    ]
+    slot_query = jnp.dot(pick_ref[...], query[...], preferred_element_type=F32).astype(BF16)
     scores = [
-        lax.dot_general(
-            query[pl.ds(pl.multiple_of(sources[slot] * heads, heads), heads), :],
-            cache_ref[slot, :, :dim],
-            (((1,), (1,)), ((), ())),
+        jnp.dot(
+            slot_query[slot * heads : (slot + 1) * heads, :],
+            key_ref[slot, :, :],
             preferred_element_type=F32,
         )
         for slot in range(slots)
     ]
+    token = lax.broadcasted_iota(jnp.int32, (heads, tokens), 1)
+    lives = [
+        jnp.concatenate([live_ref[slot * heads : (slot + 1) * heads, :]] * (tokens // LANES), axis=1)
+        for slot in range(slots)
+    ]
     masked = [jnp.where(token < lives[slot], scores[slot] * scale, EMPTY) for slot in range(slots)]
     maxima = [jnp.max(masked[slot], axis=1, keepdims=True) for slot in range(slots)]
+    starts = place_ref[:1, :]
+    places = [pl.ds(pl.multiple_of(starts[0, slot], heads), heads) for slot in range(slots)]
     for slot in range(slots):
         top[places[slot], :] = jnp.maximum(top[places[slot], :], maxima[slot])
     weights = [jnp.exp(masked[slot] - maxima[slot]) for slot in range(slots)]
@@ -195,13 +218,36 @@
     return lax.ppermute(x, "req", [(place, place ^ distance) for place in range(size)])
 
 
-def attend(requests, parts, cache, slot_request, slot_block, cache_lengths):
+def slot_tables(heads, tokens, slot_request, slot_block, cache_lengths):
+    slots = slot_request.shape[0]
+    return pl.pallas_call(
+        functools.partial(slots_kernel, tokens=tokens),
+        out_shape=(
+            jax.ShapeDtypeStruct((8, LANES), jnp.int32),
+            jax.ShapeDtypeStruct((slots * heads, cache_lengths.shape[0] * heads), BF16),
+            jax.ShapeDtypeStruct((slots * heads, LANES), jnp.int32),
+        ),
+        in_specs=[SMEM] * 3,
+        out_specs=(VMEM,) * 3,
+        compiler_params=pltpu.CompilerParams(vmem_limit_bytes=4 * MIB),
+    )(slot_request, slot_block, cache_lengths)
+
+
+def transposed_keys(cache):
+    slots, tokens, lanes = cache.shape
+    return call(
+        keys_kernel, (slots, lanes // 2, tokens), BF16, [VMEM], limit=16 * MIB,
+        moved=2 * slots * tokens * lanes,
+    )(cache)
+
+
+def attend(requests, first, second, keys, cache, place, pick, live):
     slots, tokens, lanes = cache.shape
     dim = lanes // 2
-    heads = (parts.shape[2] - lanes) // dim
+    heads = (first.shape[1] - lanes) // dim
     rows = requests * heads
     return call(
-        attend_kernel, (dim + 8, rows), F32, [SMEM] * 3 + [VMEM] * 2,
+        attend_kernel, (dim + 8, rows), F32, [VMEM] * 7,
         [
             pltpu.VMEM((rows, dim), F32),
             pltpu.VMEM((rows, dim), BF16),
@@ -214,7 +260,11 @@
         limit=16 * MIB,
         flops=2 * slots * tokens * heads * lanes,
         moved=2 * slots * tokens * lanes,
-    )(slot_request, slot_block, cache_lengths, parts, cache)
+    )(place, pick, live, first, second, keys, cache)
+
+
+def swapped(x):
+    return lax.ppermute(x, "kv", [(0, 1), (1, 0)])
 
 
 def on_device(
@@ -236,32 +286,54 @@
     columns = lax.all_to_all(
         scaled.reshape(requests, feature_rows // LANES, LANES), "req", 0, 0, tiled=True
     )
+    near = min(4, requests)
+    groups = [list(range(at, at + near)) for at in range(0, requests, near)]
     sums = call(
-        project_kernel, (requests, head_width + lanes), F32, [VMEM] * 4, limit=16 * MIB,
+        project_kernel, (near, requests, head_width + lanes), F32, [VMEM] * 4, limit=16 * MIB,
         flops=2 * requests * feature_rows * (head_width + lanes),
         moved=2 * feature_rows * (head_width + lanes),
     )(columns, norm_gain.reshape(shape), query_weight, pair_weight)
     near = min(4, requests)
     groups = [list(range(at, at + near)) for at in range(0, requests, near)]
 
-    def far_then_near(x, combine, combine_and_copy):
+    def crossed(x, distance):
+        places = [(core, place) for core in range(2) for place in range(requests)]
+        pairs = [
+            (core * requests + place, (1 - core) * requests + (place ^ distance))
+            for core, place in places
+        ]
+        return lax.ppermute(x, ("kv", "req"), pairs)
+
+    def far_then_near(x, combine, cross):
         distance = requests // 2
-        while distance > near:
-            x = combine(x, exchanged(x, distance, requests))
+        while distance >= near:
+            if cross and distance == requests // 2:
+                other = crossed(x, distance)
+                x = swapped(x)
+            else:
+                other = exchanged(x, distance, requests)
+            x = combine(x, other, near if distance == near else 1)
             distance //= 2
-        x = combine_and_copy(x, exchanged(x, distance, requests))
         return lax.all_to_all(x, "req", 0, 0, tiled=True, axis_index_groups=groups)
 
-    sums = far_then_near(
-        sums, lambda x, y: x + y,
-        lambda x, y: call(spread_sum_kernel, (near,) + x.shape, F32, [VMEM] * 2)(x, y),
-    )
-    part = attend(requests, sums, cache[0], slot_request, slot_block, cache_lengths)
-
     def merge(x, y, copies):
-        return call(merge_kernel, (copies,) + x.shape, F32, [VMEM] * 2, moved=16 * MIB)(x, y)
-
-    parts = far_then_near(part, lambda x, y: merge(x, y, 1)[0], lambda x, y: merge(x, y, near))
+        y = call(merge_kernel, (copies,) + x.shape, F32, [VMEM] * 2, moved=16 * MIB)(x, y)
+        return y if copies > 1 else y[0]
+
+    sums = lax.all_to_all(sums, "req", 0, 0, tiled=True, axis_index_groups=groups)
+    sums = call(sum_kernel, sums.shape[1:], F32, [VMEM])(sums)
+    distance = near
+    while distance < requests:
+        other = exchanged(sums, distance, requests)
+        distance *= 2
+        if distance < requests:
+            sums = sums + other
+    tables = slot_tables(
+        head_width // dim, cache.shape[2], slot_request, slot_block, cache_lengths
+    )
+    keys = transposed_keys(cache[0])
+    part = attend(requests, sums, other, keys, cache[0], *tables)
+    parts = far_then_near(part, merge, True)
 
     columns_out = w_out.shape[2]
     projected = call(
@@ -270,8 +342,8 @@
         limit=16 * MIB,
         flops=2 * requests * head_width * columns_out,
         moved=2 * head_width * columns_out,
-    )(parts, w_out[0])
-    other = lax.ppermute(projected, "kv", [(0, 1), (1, 0)])
+    )(parts, swapped(w_out[0]))
+    other = swapped(projected)
     total = call(round_sum_kernel, projected.shape, BF16, [VMEM] * 2)(projected, other)
     result = lax.all_to_all(
         total.reshape(requests, columns_out // LANES, LANES), "req", 0, 0, tiled=True

time: 60.3 us -> 58.7 us (0.973)
  waiting for transfers between devices: 12 us -> 9.94 us
  Pallas kernels: 5.03 us -> 5.78 us
    all_to_all x2 -> x1, blocking collectives: 17 us -> 8.48 us  [far_then_near(): return lax.all_to_all(x, 'req', 0, 0, tiled=True, axis_index_groups=groups)]
    all_to_all x0 -> x1, blocking collectives: none -> 8.52 us  [on_device(): lax.all_to_all(sums, 'req', 0, 0, tiled=True, axis_index_groups=groups)]
    ppermute x2 -> x1, waiting for transfers between devices: 10.7 us -> 4.01 us  [exchanged(): lax.ppermute(x, 'req', [(place, place ^ distance) for place in range(size)])]
    ppermute x1 -> x4, waiting for transfers between devices: 1.25 us -> 5.93 us  [the longest x1 4.67 us: crossed(): return lax.ppermute(x, ('kv', 'req'), pairs)]
    pallas_call x3 -> x5, Pallas kernels: 3.54 us -> 4.29 us  [the longest x1 1.43 us: attend(): call(attend_kernel, (dim + 8, rows), F32, [VMEM] * 7, [pltpu.VMEM((rows,...]
  transfers between devices with their start and end apart: 3 -> 5, of which waited for: 3 -> 3; matrix products, arithmetic and copies ran while one was open for 0% -> 0% of each run, Pallas kernels for 0% -> 8%
where the time goes in v4:
time: 58.7 us; the launch traced here: 58.4 us
  blocking collectives  39.9 us (68%)
  waiting for transfers between devices  9.94 us (17%)
  Pallas kernels  5.78 us (10%)
  local copies, waits for them, and re-layouts  1.53 us (3%)
  starting transfers between devices  1.14 us (2%)
    all_to_all x1, blocking collectives, on_device(): lax.all_to_all(scaled.reshape(requests, feature_rows // LANES, LANES), 'r...  13.8 us
    all_to_all x1, blocking collectives, on_device(): lax.all_to_all(total.reshape(requests, columns_out // LANES, LANES), 'req...  9.11 us
    all_to_all x1, blocking collectives, on_device(): lax.all_to_all(sums, 'req', 0, 0, tiled=True, axis_index_groups=groups)  8.52 us
    all_to_all x1, blocking collectives, far_then_near(): return lax.all_to_all(x, 'req', 0, 0, tiled=True, axis_index_groups=groups)  8.48 us
    ppermute x1, waiting for transfers between devices, crossed(): return lax.ppermute(x, ('kv', 'req'), pairs)  4.67 us
    ppermute x1, waiting for transfers between devices, exchanged(): lax.ppermute(x, 'req', [(place, place ^ distance) for place in range(size)])  4.01 us
    pallas_call x1, Pallas kernels, attend(): call(attend_kernel, (dim + 8, rows), F32, [VMEM] * 7, [pltpu.VMEM((rows,...  1.43 us
    pallas_call x1, Pallas kernels, on_device(): call(project_kernel, (near, requests, head_width + lanes), F32, [VMEM] *...  1.34 us
  transfers between devices with their start and end apart: 5, of which 3 were waited for; matrix products, arithmetic and copies ran while one was open for 0% of the time, Pallas kernels for 8%

profile of v4, /device:TPU:0, one launch (start us, length us, event | category | flops | bytes accessed | tf_op | source)
XLA Modules:
  0.0 58.4 jit_solution(6893238592205104110)
XLA Ops:
  0.0 0.5 collective-permute-start.3
  0.5 0.0 copy-start.3
  0.5 0.8 %copy-done.3 = bf16[1,16384]{1,0:T(2,128)(2,1)S(1)} copy-done((bf16[1,16384]{1,0:T(2,128)(2,1)S(1)}, bf16[1,16384]{1,0:T(2,128)(2,1)}, u32[]{:S(2)}) %copy-start.3) | copy-done | bytes 32792
  1.3 0.0 slice-start
  1.3 0.0 copy-start
  1.4 0.0 copy-start.1
  1.4 0.0 copy-start.2
  1.4 0.0 slice-start.1
  1.4 0.1 shard_map.93
  1.5 13.8 %all_to_all.20.x_ref = f32[8,16,128]{2,1,0:T(8,128)S(1)} all-to-all(f32[8,16,128]{2,1,0:T(8,128)S(1)} %bitcast.15), channel_id=1, replica_groups=mesh['parts'=2,'kv'=2,'req'=8] {'req'}, dimensions={0} | all-to-all | bytes 131072 | tf_op jit(solution)/shard_map/all_to_all | solution.py:286
  15.3 0.0 copy-done
  15.3 0.0 copy-done.1
  15.3 0.0 copy-done.2
  15.3 0.0 copy-start.4
  15.3 0.0 copy-start.5
  15.3 0.0 copy-start.6
  15.3 1.3 %shard_map.94 = f32[4,8,2304]{2,1,0:T(8,128)S(1)} custom-call(f32[8,16,128]{2,1,0:T(8,128)S(1)} %all_to_all.20.x_ref, f32[128,128]{1,0:T(8,128)S(1)} %bitcast.14, bf16[2048,2048]{1,0:T(8,128)(2,1)S(1)} %bitcast.11, bf16[2048,256]{1,0:T(8,128)(2,1)S(1)} %bitcast.12), custom_call_target="tpu_custom_call" | custom-call | flops 75497472 | bytes 9437184 | tf_op jit(solution)/shard_map/pallas_call | solution.py:291
  16.7 8.5 %all_to_all.21.parts_ref = f32[4,8,2304]{2,1,0:T(8,128)S(1)} all-to-all(f32[4,8,2304]{2,1,0:T(8,128)S(1)} %shard_map.94), channel_id=1, replica_groups={{0,1,2,3},{4,5,6,7},{8,9,10,11},{12,13,14,15},{16,17,18,19},{20,21,22,2..., dimensions={0} | all-to-all | bytes 589824 | tf_op jit(solution)/shard_map/all_to_all | solution.py:323
  25.2 0.5 collective-permute-start
  25.8 0.0 slice-done
  25.8 0.0 slice-done.1
  25.8 0.9 %shard_map.96.key_ref = bf16[24,128,512]{2,1,0:T(8,128)(2,1)S(1)} custom-call(bf16[24,512,256]{2,1,0:T(8,128)(2,1)S(1)} %bitcast.9), custom_call_target="tpu_custom_call" | custom-call | bytes 6291456 | tf_op jit(solution)/shard_map/pallas_call | solution.py:238
  26.6 0.0 copy-done.4
  26.6 0.0 copy-done.5
  26.7 0.0 copy-done.6
  26.7 0.6 %shard_map.91 = (s32[8,128]{1,0:T(8,128)S(1)}, bf16[384,128]{1,0:T(8,128)(2,1)S(1)}, s32[384,128]{1,0:T(8,128)S(1)}) custom-call(s32[24]{0:T(128)S(1)} %copy-done.4, s32[24]{0:T(128)S(1)} %copy-done.5, s32[8]{0:T(128)S(1)} %copy-done.6), custom_call_target="tpu_custom_call" | custom-call | tf_op jit(solution)/shard_map/pallas_call | solution.py:223
  27.3 4.0 %collective-permute-done.second_ref = f32[8,2304]{1,0:T(8,128)S(1)} collective-permute-done((f32[8,2304]{1,0:T(8,128)S(1)}, f32[8,2304]{1,0:T(8,128)S(1)}, u32[]{:S(2)}, u32[]{:S(2)}) %collective-permute-start) | collective-permute-done | bytes 73760 | tf_op jit(solution)/shard_map/ppermute | solution.py:218
  31.3 1.4 %shard_map.97 = f32[136,128]{1,0:T(8,128)S(1)} custom-call(s32[8,128]{1,0:T(8,128)S(1)} %get-tuple-element.8.place_ref, bf16[384,128]{1,0:T(8,128)(2,1)S(1)} %get-tuple-element.9.pick_ref, s32[384,128]{1,0:T(8,128)S(1)} %get-tuple-element.10.live_ref, f32[8,2304]{1,0:T(8,128)S(1)} %shard_map.95.first_ref, f32[8,2304]{1,0:T(8,128)S(1)} %collective-permute-done.second_ref, ...), custom_call_target="tpu_custom_call" | custom-call | flops 100663296 | bytes 6291456 | tf_op jit(solution)/shard_map/pallas_call | solution.py:249
  32.8 0.1 collective-permute-start.2
  32.8 0.1 collective-permute-start.1
  32.9 4.7 %collective-permute-done.2.second_ref = f32[136,128]{1,0:T(8,128)S(1)} collective-permute-done((f32[136,128]{1,0:T(8,128)S(1)}, f32[136,128]{1,0:T(8,128)S(1)}, u32[]{:S(2)}, u32[]{:S(2)}) %collective-permute-start.2) | collective-permute-done | bytes 69664 | tf_op jit(solution)/shard_map/ppermute | solution.py:305
  37.6 0.0 collective-permute-done.1.first_ref
  37.6 8.5 %all_to_all.22.parts_ref = f32[4,136,128]{2,1,0:T(8,128)S(1)} all-to-all(f32[4,136,128]{2,1,0:T(8,128)S(1)} %shard_map.98), channel_id=1, replica_groups={{0,1,2,3},{4,5,6,7},{8,9,10,11},{12,13,14,15},{16,17,18,19},{20,21,22,2..., dimensions={0} | all-to-all | bytes 557056 | tf_op jit(solution)/shard_map/all_to_all | solution.py:317
  46.1 0.0 collective-permute-done.3.weight_ref
  46.1 1.3 %shard_map.99.first_ref = f32[128,128]{1,0:T(8,128)S(1)} custom-call(f32[4,136,128]{2,1,0:T(8,128)S(1)} %all_to_all.22.parts_ref, bf16[2048,2048]{1,0:T(8,128)(2,1)S(1)} %collective-permute-done.3.weight_ref), custom_call_target="tpu_custom_call" | custom-call | flops 67108864 | bytes 8388608 | tf_op jit(solution)/shard_map/pallas_call | solution.py:339
  47.4 0.0 collective-permute-start.4
  47.4 1.2 %collective-permute-done.4.second_ref = f32[128,128]{1,0:T(8,128)S(1)} collective-permute-done((f32[128,128]{1,0:T(8,128)S(1)}, f32[128,128]{1,0:T(8,128)S(1)}, u32[]{:S(2)}, u32[]{:S(2)}) %collective-permute-start.4) | collective-permute-done | bytes 65568 | tf_op jit(solution)/shard_map/ppermute | solution.py:267
  48.7 9.1 %all_to_all.23 = bf16[8,16,128]{2,1,0:T(8,128)(2,1)S(1)} all-to-all(bf16[8,16,128]{2,1,0:T(8,128)(2,1)S(1)} %bitcast.13), channel_id=1, replica_groups=mesh['parts'=2,'kv'=2,'req'=8] {'req'}, dimensions={0} | all-to-all | bytes 65536 | tf_op jit(solution)/shard_map/all_to_all | solution.py:348
  57.8 0.6 %reshape.23 = bf16[1,16384]{1,0:T(2,128)(2,1)} reshape(bf16[8,16,128]{2,1,0:T(8,128)(2,1)S(1)} %all_to_all.23) | data formatting | bytes 65536 | tf_op jit(solution)/shard_map/reshape | solution.py:351
  (5 shorter events, 0.1 us)
Async XLA Ops:
  0.0 46.1 %collective-permute-start.3 = (bf16[2048,2048]{1,0:T(8,128)(2,1)}, bf16[2048,2048]{1,0:T(8,128)(2,1)S(1)}, u32[]{:S(2)}, u32[]{:S(2)}) collective-permute-start(bf16[2048,2048]{1,0:T(8,128)(2,1)} %bitcast.16), channel_id=1, source_target_pairs={{0,8},{8,0},{1,9},{9,1},{2,10},{10,2},{3,11},{11,3},{4,12},{12,4},... | collective-permute-start | bytes 25165832 | tf_op jit(solution)/shard_map/ppermute | solution.py:267
  0.5 0.8 %copy-start.3 = (bf16[1,16384]{1,0:T(2,128)(2,1)S(1)}, bf16[1,16384]{1,0:T(2,128)(2,1)}, u32[]{:S(2)}) copy-start(bf16[1,16384]{1,0:T(2,128)(2,1)} %hidden_ref.1) | copy-start | bytes 98308
  1.3 24.5 %slice-start = ((s8[6291456]{0:T(1024)(128)(4,1)}), s8[4194304]{0:T(1024)(128)(4,1)S(1)}, s32[]{:S(2)}) async-start(s8[6291456]{0:T(1024)(128)(4,1)} %bitcast.7), calls=%async_computation.4 | async-start | bytes 8388608
  1.3 14.0 %copy-start = (bf16[2048,1,2048]{2,0,1:T(8,128)(2,1)S(1)}, bf16[2048,1,2048]{2,0,1:T(8,128)(2,1)}, u32[]{:S(2)}) copy-start(bf16[2048,1,2048]{2,0,1:T(8,128)(2,1)} %param.11) | copy-start | bytes 25165828
  1.4 13.9 %copy-start.1 = (bf16[2048,1,256]{2,0,1:T(8,128)(2,1)S(1)}, bf16[2048,1,256]{2,0,1:T(8,128)(2,1)}, u32[]{:S(2)}) copy-start(bf16[2048,1,256]{2,0,1:T(8,128)(2,1)} %param.12) | copy-start | bytes 3145732
  1.4 13.9 %copy-start.2 = (f32[16384]{0:T(1024)S(1)}, f32[16384]{0:T(1024)}, u32[]{:S(2)}) copy-start(f32[16384]{0:T(1024)} %param.10) | copy-start | bytes 196612
  1.4 24.4 %slice-start.1 = ((s8[6291456]{0:T(1024)(128)(4,1)}), s8[2097152]{0:T(1024)(128)(4,1)S(1)}, s32[]{:S(2)}) async-start(s8[6291456]{0:T(1024)(128)(4,1)} %bitcast.7), calls=%async_computation.5 | async-start | bytes 4194304
  15.3 11.3 %copy-start.4 = (s32[24]{0:T(128)S(1)}, s32[24]{0:T(128)}, u32[]{:S(2)}) copy-start(s32[24]{0:T(128)} %owner_ref.1) | copy-start | bytes 292
  15.3 11.3 %copy-start.5 = (s32[24]{0:T(128)S(1)}, s32[24]{0:T(128)}, u32[]{:S(2)}) copy-start(s32[24]{0:T(128)} %block_ref.1) | copy-start | bytes 292
  15.3 11.3 %copy-start.6 = (s32[8]{0:T(128)S(1)}, s32[8]{0:T(128)}, u32[]{:S(2)}) copy-start(s32[8]{0:T(128)} %length_ref.1) | copy-start | bytes 100
  25.2 6.1 %collective-permute-start = (f32[8,2304]{1,0:T(8,128)S(1)}, f32[8,2304]{1,0:T(8,128)S(1)}, u32[]{:S(2)}, u32[]{:S(2)}) collective-permute-start(f32[8,2304]{1,0:T(8,128)S(1)} %shard_map.95.first_ref), channel_id=1, source_target_pairs={{0,4},{1,5},{2,6},{3,7},{4,0},{5,1},{6,2},{7,3},{8,12},{9,13},{10,... | collective-permute-start | bytes 221192 | tf_op jit(solution)/shard_map/ppermute | solution.py:218
  32.8 4.8 %collective-permute-start.2 = (f32[136,128]{1,0:T(8,128)S(1)}, f32[136,128]{1,0:T(8,128)S(1)}, u32[]{:S(2)}, u32[]{:S(2)}) collective-permute-start(f32[136,128]{1,0:T(8,128)S(1)} %shard_map.97), channel_id=1, source_target_pairs={{0,12},{1,13},{2,14},{3,15},{4,8},{5,9},{6,10},{7,11},{8,4},{9,5},... | collective-permute-start | bytes 208904 | tf_op jit(solution)/shard_map/ppermute | solution.py:305
  32.8 4.8 %collective-permute-start.1 = (f32[136,128]{1,0:T(8,128)S(1)}, f32[136,128]{1,0:T(8,128)S(1)}, u32[]{:S(2)}, u32[]{:S(2)}) collective-permute-start(f32[136,128]{1,0:T(8,128)S(1)} %shard_map.97), channel_id=1, source_target_pairs={{0,8},{8,0},{1,9},{9,1},{2,10},{10,2},{3,11},{11,3},{4,12},{12,4},... | collective-permute-start | bytes 208904 | tf_op jit(solution)/shard_map/ppermute | solution.py:267
  47.4 1.3 %collective-permute-start.4 = (f32[128,128]{1,0:T(8,128)S(1)}, f32[128,128]{1,0:T(8,128)S(1)}, u32[]{:S(2)}, u32[]{:S(2)}) collective-permute-start(f32[128,128]{1,0:T(8,128)S(1)} %shard_map.99.first_ref), channel_id=1, source_target_pairs={{0,8},{8,0},{1,9},{9,1},{2,10},{10,2},{3,11},{11,3},{4,12},{12,4},... | collective-permute-start | bytes 196616 | tf_op jit(solution)/shard_map/ppermute | solution.py:267

commit v5 on v4

--- a/solution.py
+++ b/solution.py
@@ -40,8 +40,12 @@
         for copy in range(out_ref.shape[0]):
             out_ref[copy, :, at : at + step] = y
     y = jnp.dot(x, pair_ref[...], preferred_element_type=F32)
-    for copy in range(out_ref.shape[0]):
-        out_ref[copy, :, width:] = y
+    near, requests = out_ref.shape[:2]
+    unused = jnp.zeros((requests - 2 * (requests // near), LANES), F32)
+    for copy in range(near):
+        wanted = [y[at : at + 1, :] for at in range(copy, requests, near)]
+        pairs = [row[:, :LANES] for row in wanted] + [row[:, LANES:] for row in wanted]
+        out_ref[copy, :, width:] = jnp.concatenate(pairs + [unused], axis=0)
 
 
 def sum_kernel(parts_ref, out_ref):
@@ -80,12 +84,12 @@
 
 def attend_kernel(
     place_ref, pick_ref, live_ref, first_ref, second_ref, key_ref, cache_ref, out_ref,
-    wide, query, new_key, new_value, top, total, summed,
+    wide, query, new_pair, top, total, summed,
 ):
     requests, width = first_ref.shape
     slots, tokens, lanes = cache_ref.shape
     dim = lanes // 2
-    heads = (width - lanes) // dim
+    heads = width // dim - 1
 
     def summed_parts(at):
         return first_ref[:, at] + second_ref[:, at]
@@ -96,14 +100,13 @@
         at = slice(head * dim, (head + 1) * dim)
         wide[pl.ds(head, requests, stride=heads), :] = summed_parts(at)
     query[...] = wide[...].astype(BF16)
-    for new, start in ((new_key, heads * dim), (new_value, heads * dim + dim)):
-        at = slice(start, start + dim)
-        new[...] = summed_parts(at).astype(BF16).astype(F32)
+    new_pair[...] = summed_parts(slice(heads * dim, width)).astype(BF16).astype(F32)
 
     me = lax.axis_index("req").astype(jnp.int32)
     mine = pl.ds(pl.multiple_of(me * heads, heads), heads)
-    own_key = new_key[pl.ds(me, 1), :]
-    own_value = new_value[pl.ds(me, 1), :]
+    near = min(4, requests)
+    own_key = new_pair[pl.ds(me // near, 1), :]
+    own_value = new_pair[pl.ds(requests // near + me // near, 1), :]
     own_score = (
         jnp.sum(query[mine, :].astype(F32) * own_key, axis=1, keepdims=True) * scale
     )
@@ -148,8 +151,8 @@
     summed[mine, :] = summed[mine, :] + own_factor * own_value
 
     out_ref[:dim, :] = summed[:rows, :].T
-    out_ref[dim : dim + 1, :] = top[:rows, :].T[:1, :]
-    out_ref[dim + 1 : dim + 2, :] = total[:rows, :].T[:1, :]
+    lane = lax.broadcasted_iota(jnp.int32, (rows, dim), 1)
+    out_ref[dim : dim + 2, :] = jnp.where(lane == 0, top[:rows, :], total[:rows, :]).T[:2, :]
     out_ref[dim + 2 :, :] = jnp.zeros((out_ref.shape[0] - dim - 2, rows), F32)
 
 
@@ -244,14 +247,13 @@
 def attend(requests, first, second, keys, cache, place, pick, live):
     slots, tokens, lanes = cache.shape
     dim = lanes // 2
-    heads = (first.shape[1] - lanes) // dim
+    heads = first.shape[1] // dim - 1
     rows = requests * heads
     return call(
         attend_kernel, (dim + 8, rows), F32, [VMEM] * 7,
         [
             pltpu.VMEM((rows, dim), F32),
             pltpu.VMEM((rows, dim), BF16),
-            pltpu.VMEM((requests, dim), F32),
             pltpu.VMEM((requests, dim), F32),
             pltpu.VMEM((rows + heads, dim), F32),
             pltpu.VMEM((rows + heads, dim), F32),
@@ -289,7 +291,7 @@
     near = min(4, requests)
     groups = [list(range(at, at + near)) for at in range(0, requests, near)]
     sums = call(
-        project_kernel, (near, requests, head_width + lanes), F32, [VMEM] * 4, limit=16 * MIB,
+        project_kernel, (near, requests, head_width + dim), F32, [VMEM] * 4, limit=16 * MIB,
         flops=2 * requests * feature_rows * (head_width + lanes),
         moved=2 * feature_rows * (head_width + lanes),
     )(columns, norm_gain.reshape(shape), query_weight, pair_weight)

time: 58.7 us -> 58.6 us (level)
  no operation moved by 1% of the time
where the time goes in v5:
time: 58.6 us; the launch traced here: 58.3 us
  blocking collectives  39.9 us (68%)
  waiting for transfers between devices  9.86 us (17%)
  Pallas kernels  5.74 us (10%)
  local copies, waits for them, and re-layouts  1.53 us (3%)
  starting transfers between devices  1.14 us (2%)
    all_to_all x1, blocking collectives, on_device(): lax.all_to_all(scaled.reshape(requests, feature_rows // LANES, LANES), 'r...  13.8 us
    all_to_all x1, blocking collectives, on_device(): lax.all_to_all(total.reshape(requests, columns_out // LANES, LANES), 'req...  9.12 us
    all_to_all x1, blocking collectives, far_then_near(): return lax.all_to_all(x, 'req', 0, 0, tiled=True, axis_index_groups=groups)  8.48 us
    all_to_all x1, blocking collectives, on_device(): lax.all_to_all(sums, 'req', 0, 0, tiled=True, axis_index_groups=groups)  8.47 us
    ppermute x1, waiting for transfers between devices, crossed(): return lax.ppermute(x, ('kv', 'req'), pairs)  4.68 us
    ppermute x1, waiting for transfers between devices, exchanged(): lax.ppermute(x, 'req', [(place, place ^ distance) for place in range(size)])  3.92 us
    pallas_call x1, Pallas kernels, attend(): call(attend_kernel, (dim + 8, rows), F32, [VMEM] * 7, [pltpu.VMEM((rows,...  1.39 us
    pallas_call x1, Pallas kernels, on_device(): call(project_kernel, (near, requests, head_width + dim), F32, [VMEM] * 4,...  1.34 us
  transfers between devices with their start and end apart: 5, of which 3 were waited for; matrix products, arithmetic and copies ran while one was open for 0% of the time, Pallas kernels for 8%

profile of v5, /device:TPU:0, one launch (start us, length us, event | category | flops | bytes accessed | tf_op | source)
XLA Modules:
  0.0 58.3 jit_solution(15480226040118365395)
XLA Ops:
  0.0 0.5 collective-permute-start.3
  0.5 0.0 copy-start.3
  0.5 0.8 %copy-done.3 = bf16[1,16384]{1,0:T(2,128)(2,1)S(1)} copy-done((bf16[1,16384]{1,0:T(2,128)(2,1)S(1)}, bf16[1,16384]{1,0:T(2,128)(2,1)}, u32[]{:S(2)}) %copy-start.3) | copy-done | bytes 32792
  1.3 0.0 slice-start
  1.3 0.0 copy-start
  1.4 0.0 copy-start.1
  1.4 0.0 copy-start.2
  1.4 0.0 slice-start.1
  1.4 0.1 shard_map.93
  1.5 13.8 %all_to_all.20.x_ref = f32[8,16,128]{2,1,0:T(8,128)S(1)} all-to-all(f32[8,16,128]{2,1,0:T(8,128)S(1)} %bitcast.15), channel_id=1, replica_groups=mesh['parts'=2,'kv'=2,'req'=8] {'req'}, dimensions={0} | all-to-all | bytes 131072 | tf_op jit(solution)/shard_map/all_to_all | solution.py:288
  15.3 0.0 copy-done
  15.3 0.0 copy-done.1
  15.3 0.0 copy-done.2
  15.3 0.0 copy-start.4
  15.3 0.0 copy-start.5
  15.3 0.0 copy-start.6
  15.3 1.3 %shard_map.94 = f32[4,8,2176]{2,1,0:T(8,128)S(1)} custom-call(f32[8,16,128]{2,1,0:T(8,128)S(1)} %all_to_all.20.x_ref, f32[128,128]{1,0:T(8,128)S(1)} %bitcast.14, bf16[2048,2048]{1,0:T(8,128)(2,1)S(1)} %bitcast.11, bf16[2048,256]{1,0:T(8,128)(2,1)S(1)} %bitcast.12), custom_call_target="tpu_custom_call" | custom-call | flops 75497472 | bytes 9437184 | tf_op jit(solution)/shard_map/pallas_call | solution.py:293
  16.7 8.5 %all_to_all.21.parts_ref = f32[4,8,2176]{2,1,0:T(8,128)S(1)} all-to-all(f32[4,8,2176]{2,1,0:T(8,128)S(1)} %shard_map.94), channel_id=1, replica_groups={{0,1,2,3},{4,5,6,7},{8,9,10,11},{12,13,14,15},{16,17,18,19},{20,21,22,2..., dimensions={0} | all-to-all | bytes 557056 | tf_op jit(solution)/shard_map/all_to_all | solution.py:325
  25.2 0.5 collective-permute-start
  25.7 0.0 slice-done
  25.7 0.0 slice-done.1
  25.7 0.9 %shard_map.96.key_ref = bf16[24,128,512]{2,1,0:T(8,128)(2,1)S(1)} custom-call(bf16[24,512,256]{2,1,0:T(8,128)(2,1)S(1)} %bitcast.9), custom_call_target="tpu_custom_call" | custom-call | bytes 6291456 | tf_op jit(solution)/shard_map/pallas_call | solution.py:241
  26.6 0.0 copy-done.4
  26.6 0.0 copy-done.5
  26.6 0.0 copy-done.6
  26.6 0.6 %shard_map.91 = (s32[8,128]{1,0:T(8,128)S(1)}, bf16[384,128]{1,0:T(8,128)(2,1)S(1)}, s32[384,128]{1,0:T(8,128)S(1)}) custom-call(s32[24]{0:T(128)S(1)} %copy-done.4, s32[24]{0:T(128)S(1)} %copy-done.5, s32[8]{0:T(128)S(1)} %copy-done.6), custom_call_target="tpu_custom_call" | custom-call | tf_op jit(solution)/shard_map/pallas_call | solution.py:226
  27.3 3.9 %collective-permute-done.second_ref = f32[8,2176]{1,0:T(8,128)S(1)} collective-permute-done((f32[8,2176]{1,0:T(8,128)S(1)}, f32[8,2176]{1,0:T(8,128)S(1)}, u32[]{:S(2)}, u32[]{:S(2)}) %collective-permute-start) | collective-permute-done | bytes 69664 | tf_op jit(solution)/shard_map/ppermute | solution.py:221
  31.2 1.4 %shard_map.97 = f32[136,128]{1,0:T(8,128)S(1)} custom-call(s32[8,128]{1,0:T(8,128)S(1)} %get-tuple-element.8.place_ref, bf16[384,128]{1,0:T(8,128)(2,1)S(1)} %get-tuple-element.9.pick_ref, s32[384,128]{1,0:T(8,128)S(1)} %get-tuple-element.10.live_ref, f32[8,2176]{1,0:T(8,128)S(1)} %shard_map.95.first_ref, f32[8,2176]{1,0:T(8,128)S(1)} %collective-permute-done.second_ref, ...), custom_call_target="tpu_custom_call" | custom-call | flops 100663296 | bytes 6291456 | tf_op jit(solution)/shard_map/pallas_call | solution.py:252
  32.6 0.1 collective-permute-start.2
  32.7 0.1 collective-permute-start.1
  32.7 4.7 %collective-permute-done.2.second_ref = f32[136,128]{1,0:T(8,128)S(1)} collective-permute-done((f32[136,128]{1,0:T(8,128)S(1)}, f32[136,128]{1,0:T(8,128)S(1)}, u32[]{:S(2)}, u32[]{:S(2)}) %collective-permute-start.2) | collective-permute-done | bytes 69664 | tf_op jit(solution)/shard_map/ppermute | solution.py:307
  37.4 0.0 collective-permute-done.1.first_ref
  37.5 8.5 %all_to_all.22.parts_ref = f32[4,136,128]{2,1,0:T(8,128)S(1)} all-to-all(f32[4,136,128]{2,1,0:T(8,128)S(1)} %shard_map.98), channel_id=1, replica_groups={{0,1,2,3},{4,5,6,7},{8,9,10,11},{12,13,14,15},{16,17,18,19},{20,21,22,2..., dimensions={0} | all-to-all | bytes 557056 | tf_op jit(solution)/shard_map/all_to_all | solution.py:319
  45.9 0.0 collective-permute-done.3.weight_ref
  46.0 1.3 %shard_map.99.first_ref = f32[128,128]{1,0:T(8,128)S(1)} custom-call(f32[4,136,128]{2,1,0:T(8,128)S(1)} %all_to_all.22.parts_ref, bf16[2048,2048]{1,0:T(8,128)(2,1)S(1)} %collective-permute-done.3.weight_ref), custom_call_target="tpu_custom_call" | custom-call | flops 67108864 | bytes 8388608 | tf_op jit(solution)/shard_map/pallas_call | solution.py:341
  47.2 0.0 collective-permute-start.4
  47.3 1.2 %collective-permute-done.4.second_ref = f32[128,128]{1,0:T(8,128)S(1)} collective-permute-done((f32[128,128]{1,0:T(8,128)S(1)}, f32[128,128]{1,0:T(8,128)S(1)}, u32[]{:S(2)}, u32[]{:S(2)}) %collective-permute-start.4) | collective-permute-done | bytes 65568 | tf_op jit(solution)/shard_map/ppermute | solution.py:269
  48.5 9.1 %all_to_all.23 = bf16[8,16,128]{2,1,0:T(8,128)(2,1)S(1)} all-to-all(bf16[8,16,128]{2,1,0:T(8,128)(2,1)S(1)} %bitcast.13), channel_id=1, replica_groups=mesh['parts'=2,'kv'=2,'req'=8] {'req'}, dimensions={0} | all-to-all | bytes 65536 | tf_op jit(solution)/shard_map/all_to_all | solution.py:350
  57.6 0.6 %reshape.23 = bf16[1,16384]{1,0:T(2,128)(2,1)} reshape(bf16[8,16,128]{2,1,0:T(8,128)(2,1)S(1)} %all_to_all.23) | data formatting | bytes 65536 | tf_op jit(solution)/shard_map/reshape | solution.py:353
  (5 shorter events, 0.1 us)
Async XLA Ops:
  0.0 46.0 %collective-permute-start.3 = (bf16[2048,2048]{1,0:T(8,128)(2,1)}, bf16[2048,2048]{1,0:T(8,128)(2,1)S(1)}, u32[]{:S(2)}, u32[]{:S(2)}) collective-permute-start(bf16[2048,2048]{1,0:T(8,128)(2,1)} %bitcast.16), channel_id=1, source_target_pairs={{0,8},{8,0},{1,9},{9,1},{2,10},{10,2},{3,11},{11,3},{4,12},{12,4},... | collective-permute-start | bytes 25165832 | tf_op jit(solution)/shard_map/ppermute | solution.py:269
  0.5 0.8 %copy-start.3 = (bf16[1,16384]{1,0:T(2,128)(2,1)S(1)}, bf16[1,16384]{1,0:T(2,128)(2,1)}, u32[]{:S(2)}) copy-start(bf16[1,16384]{1,0:T(2,128)(2,1)} %hidden_ref.1) | copy-start | bytes 98308
  1.3 24.4 %slice-start = ((s8[6291456]{0:T(1024)(128)(4,1)}), s8[4194304]{0:T(1024)(128)(4,1)S(1)}, s32[]{:S(2)}) async-start(s8[6291456]{0:T(1024)(128)(4,1)} %bitcast.7), calls=%async_computation.4 | async-start | bytes 8388608
  1.3 14.0 %copy-start = (bf16[2048,1,2048]{2,0,1:T(8,128)(2,1)S(1)}, bf16[2048,1,2048]{2,0,1:T(8,128)(2,1)}, u32[]{:S(2)}) copy-start(bf16[2048,1,2048]{2,0,1:T(8,128)(2,1)} %param.11) | copy-start | bytes 25165828
  1.4 13.9 %copy-start.1 = (bf16[2048,1,256]{2,0,1:T(8,128)(2,1)S(1)}, bf16[2048,1,256]{2,0,1:T(8,128)(2,1)}, u32[]{:S(2)}) copy-start(bf16[2048,1,256]{2,0,1:T(8,128)(2,1)} %param.12) | copy-start | bytes 3145732
  1.4 13.9 %copy-start.2 = (f32[16384]{0:T(1024)S(1)}, f32[16384]{0:T(1024)}, u32[]{:S(2)}) copy-start(f32[16384]{0:T(1024)} %param.10) | copy-start | bytes 196612
  1.4 24.3 %slice-start.1 = ((s8[6291456]{0:T(1024)(128)(4,1)}), s8[2097152]{0:T(1024)(128)(4,1)S(1)}, s32[]{:S(2)}) async-start(s8[6291456]{0:T(1024)(128)(4,1)} %bitcast.7), calls=%async_computation.5 | async-start | bytes 4194304
  15.3 11.3 %copy-start.4 = (s32[24]{0:T(128)S(1)}, s32[24]{0:T(128)}, u32[]{:S(2)}) copy-start(s32[24]{0:T(128)} %owner_ref.1) | copy-start | bytes 292
  15.3 11.3 %copy-start.5 = (s32[24]{0:T(128)S(1)}, s32[24]{0:T(128)}, u32[]{:S(2)}) copy-start(s32[24]{0:T(128)} %block_ref.1) | copy-start | bytes 292
  15.3 11.3 %copy-start.6 = (s32[8]{0:T(128)S(1)}, s32[8]{0:T(128)}, u32[]{:S(2)}) copy-start(s32[8]{0:T(128)} %length_ref.1) | copy-start | bytes 100
  25.2 6.0 %collective-permute-start = (f32[8,2176]{1,0:T(8,128)S(1)}, f32[8,2176]{1,0:T(8,128)S(1)}, u32[]{:S(2)}, u32[]{:S(2)}) collective-permute-start(f32[8,2176]{1,0:T(8,128)S(1)} %shard_map.95.first_ref), channel_id=1, source_target_pairs={{0,4},{1,5},{2,6},{3,7},{4,0},{5,1},{6,2},{7,3},{8,12},{9,13},{10,... | collective-permute-start | bytes 208904 | tf_op jit(solution)/shard_map/ppermute | solution.py:221
  32.6 4.8 %collective-permute-start.2 = (f32[136,128]{1,0:T(8,128)S(1)}, f32[136,128]{1,0:T(8,128)S(1)}, u32[]{:S(2)}, u32[]{:S(2)}) collective-permute-start(f32[136,128]{1,0:T(8,128)S(1)} %shard_map.97), channel_id=1, source_target_pairs={{0,12},{1,13},{2,14},{3,15},{4,8},{5,9},{6,10},{7,11},{8,4},{9,5},... | collective-permute-start | bytes 208904 | tf_op jit(solution)/shard_map/ppermute | solution.py:307
  32.7 4.8 %collective-permute-start.1 = (f32[136,128]{1,0:T(8,128)S(1)}, f32[136,128]{1,0:T(8,128)S(1)}, u32[]{:S(2)}, u32[]{:S(2)}) collective-permute-start(f32[136,128]{1,0:T(8,128)S(1)} %shard_map.97), channel_id=1, source_target_pairs={{0,8},{8,0},{1,9},{9,1},{2,10},{10,2},{3,11},{11,3},{4,12},{12,4},... | collective-permute-start | bytes 208904 | tf_op jit(solution)/shard_map/ppermute | solution.py:269
  47.2 1.3 %collective-permute-start.4 = (f32[128,128]{1,0:T(8,128)S(1)}, f32[128,128]{1,0:T(8,128)S(1)}, u32[]{:S(2)}, u32[]{:S(2)}) collective-permute-start(f32[128,128]{1,0:T(8,128)S(1)} %shard_map.99.first_ref), channel_id=1, source_target_pairs={{0,8},{8,0},{1,9},{9,1},{2,10},{10,2},{3,11},{11,3},{4,12},{12,4},... | collective-permute-start | bytes 196616 | tf_op jit(solution)/shard_map/ppermute | solution.py:269

commit v6 on v5

--- a/solution.py
+++ b/solution.py
@@ -34,7 +34,7 @@
     x = x_ref[...] * gain[None]
     x = jnp.concatenate([x[:, chunk, :] for chunk in range(chunks)], axis=1).astype(BF16)
     width = query_ref.shape[1]
-    step = 512
+    step = 1024
     for at in range(0, width, step):
         y = jnp.dot(x, query_ref[:, at : at + step], preferred_element_type=F32)
         for copy in range(out_ref.shape[0]):
@@ -193,7 +193,7 @@
     ).astype(BF16)
     width = weight_ref.shape[1]
     chunks = width // LANES
-    step = min(512, width)
+    step = min(1024, width)
     for at in range(0, width, step):
         y = jnp.dot(x, weight_ref[:, at : at + step], preferred_element_type=F32)
         for chunk in range(step // LANES):

time: 58.6 us -> 58.5 us (level)
  no operation moved by 1% of the time
where the time goes in v6:
time: 58.5 us; the launch traced here: 58.3 us
  blocking collectives  39.8 us (68%)
  waiting for transfers between devices  9.86 us (17%)
  Pallas kernels  5.74 us (10%)
  local copies, waits for them, and re-layouts  1.53 us (3%)
  starting transfers between devices  1.14 us (2%)
    all_to_all x1, blocking collectives, on_device(): lax.all_to_all(scaled.reshape(requests, feature_rows // LANES, LANES), 'r...  13.8 us
    all_to_all x1, blocking collectives, on_device(): lax.all_to_all(total.reshape(requests, columns_out // LANES, LANES), 'req...  9.1 us
    all_to_all x1, blocking collectives, far_then_near(): return lax.all_to_all(x, 'req', 0, 0, tiled=True, axis_index_groups=groups)  8.48 us
    all_to_all x1, blocking collectives, on_device(): lax.all_to_all(sums, 'req', 0, 0, tiled=True, axis_index_groups=groups)  8.47 us
    ppermute x1, waiting for transfers between devices, crossed(): return lax.ppermute(x, ('kv', 'req'), pairs)  4.68 us
    ppermute x1, waiting for transfers between devices, exchanged(): lax.ppermute(x, 'req', [(place, place ^ distance) for place in range(size)])  3.92 us
    pallas_call x1, Pallas kernels, attend(): call(attend_kernel, (dim + 8, rows), F32, [VMEM] * 7, [pltpu.VMEM((rows,...  1.39 us
    pallas_call x1, Pallas kernels, on_device(): call(project_kernel, (near, requests, head_width + dim), F32, [VMEM] * 4,...  1.34 us
  transfers between devices with their start and end apart: 5, of which 3 were waited for; matrix products, arithmetic and copies ran while one was open for 0% of the time, Pallas kernels for 8%

profile of v6, /device:TPU:0, one launch (start us, length us, event | category | flops | bytes accessed | tf_op | source)
XLA Modules:
  0.0 58.3 jit_solution(15480226040118365395)
XLA Ops:
  0.0 0.5 collective-permute-start.3
  0.5 0.0 copy-start.3
  0.5 0.8 %copy-done.3 = bf16[1,16384]{1,0:T(2,128)(2,1)S(1)} copy-done((bf16[1,16384]{1,0:T(2,128)(2,1)S(1)}, bf16[1,16384]{1,0:T(2,128)(2,1)}, u32[]{:S(2)}) %copy-start.3) | copy-done | bytes 32792
  1.3 0.0 slice-start
  1.3 0.0 copy-start
  1.4 0.0 copy-start.1
  1.4 0.0 copy-start.2
  1.4 0.0 slice-start.1
  1.4 0.1 shard_map.93
  1.5 13.8 %all_to_all.20.x_ref = f32[8,16,128]{2,1,0:T(8,128)S(1)} all-to-all(f32[8,16,128]{2,1,0:T(8,128)S(1)} %bitcast.15), channel_id=1, replica_groups=mesh['parts'=2,'kv'=2,'req'=8] {'req'}, dimensions={0} | all-to-all | bytes 131072 | tf_op jit(solution)/shard_map/all_to_all | solution.py:288
  15.3 0.0 copy-done
  15.3 0.0 copy-done.1
  15.3 0.0 copy-done.2
  15.3 0.0 copy-start.4
  15.3 0.0 copy-start.5
  15.3 0.0 copy-start.6
  15.3 1.3 %shard_map.94 = f32[4,8,2176]{2,1,0:T(8,128)S(1)} custom-call(f32[8,16,128]{2,1,0:T(8,128)S(1)} %all_to_all.20.x_ref, f32[128,128]{1,0:T(8,128)S(1)} %bitcast.14, bf16[2048,2048]{1,0:T(8,128)(2,1)S(1)} %bitcast.11, bf16[2048,256]{1,0:T(8,128)(2,1)S(1)} %bitcast.12), custom_call_target="tpu_custom_call" | custom-call | flops 75497472 | bytes 9437184 | tf_op jit(solution)/shard_map/pallas_call | solution.py:293
  16.7 8.5 %all_to_all.21.parts_ref = f32[4,8,2176]{2,1,0:T(8,128)S(1)} all-to-all(f32[4,8,2176]{2,1,0:T(8,128)S(1)} %shard_map.94), channel_id=1, replica_groups={{0,1,2,3},{4,5,6,7},{8,9,10,11},{12,13,14,15},{16,17,18,19},{20,21,22,2..., dimensions={0} | all-to-all | bytes 557056 | tf_op jit(solution)/shard_map/all_to_all | solution.py:325
  25.2 0.5 collective-permute-start
  25.7 0.0 slice-done
  25.7 0.0 slice-done.1
  25.7 0.9 %shard_map.96.key_ref = bf16[24,128,512]{2,1,0:T(8,128)(2,1)S(1)} custom-call(bf16[24,512,256]{2,1,0:T(8,128)(2,1)S(1)} %bitcast.9), custom_call_target="tpu_custom_call" | custom-call | bytes 6291456 | tf_op jit(solution)/shard_map/pallas_call | solution.py:241
  26.6 0.0 copy-done.4
  26.6 0.0 copy-done.5
  26.6 0.0 copy-done.6
  26.6 0.6 %shard_map.91 = (s32[8,128]{1,0:T(8,128)S(1)}, bf16[384,128]{1,0:T(8,128)(2,1)S(1)}, s32[384,128]{1,0:T(8,128)S(1)}) custom-call(s32[24]{0:T(128)S(1)} %copy-done.4, s32[24]{0:T(128)S(1)} %copy-done.5, s32[8]{0:T(128)S(1)} %copy-done.6), custom_call_target="tpu_custom_call" | custom-call | tf_op jit(solution)/shard_map/pallas_call | solution.py:226
  27.3 3.9 %collective-permute-done.second_ref = f32[8,2176]{1,0:T(8,128)S(1)} collective-permute-done((f32[8,2176]{1,0:T(8,128)S(1)}, f32[8,2176]{1,0:T(8,128)S(1)}, u32[]{:S(2)}, u32[]{:S(2)}) %collective-permute-start) | collective-permute-done | bytes 69664 | tf_op jit(solution)/shard_map/ppermute | solution.py:221
  31.2 1.4 %shard_map.97 = f32[136,128]{1,0:T(8,128)S(1)} custom-call(s32[8,128]{1,0:T(8,128)S(1)} %get-tuple-element.8.place_ref, bf16[384,128]{1,0:T(8,128)(2,1)S(1)} %get-tuple-element.9.pick_ref, s32[384,128]{1,0:T(8,128)S(1)} %get-tuple-element.10.live_ref, f32[8,2176]{1,0:T(8,128)S(1)} %shard_map.95.first_ref, f32[8,2176]{1,0:T(8,128)S(1)} %collective-permute-done.second_ref, ...), custom_call_target="tpu_custom_call" | custom-call | flops 100663296 | bytes 6291456 | tf_op jit(solution)/shard_map/pallas_call | solution.py:252
  32.6 0.1 collective-permute-start.2
  32.7 0.1 collective-permute-start.1
  32.8 4.7 %collective-permute-done.2.second_ref = f32[136,128]{1,0:T(8,128)S(1)} collective-permute-done((f32[136,128]{1,0:T(8,128)S(1)}, f32[136,128]{1,0:T(8,128)S(1)}, u32[]{:S(2)}, u32[]{:S(2)}) %collective-permute-start.2) | collective-permute-done | bytes 69664 | tf_op jit(solution)/shard_map/ppermute | solution.py:307
  37.4 0.0 collective-permute-done.1.first_ref
  37.5 8.5 %all_to_all.22.parts_ref = f32[4,136,128]{2,1,0:T(8,128)S(1)} all-to-all(f32[4,136,128]{2,1,0:T(8,128)S(1)} %shard_map.98), channel_id=1, replica_groups={{0,1,2,3},{4,5,6,7},{8,9,10,11},{12,13,14,15},{16,17,18,19},{20,21,22,2..., dimensions={0} | all-to-all | bytes 557056 | tf_op jit(solution)/shard_map/all_to_all | solution.py:319
  45.9 0.0 collective-permute-done.3.weight_ref
  46.0 1.3 %shard_map.99.first_ref = f32[128,128]{1,0:T(8,128)S(1)} custom-call(f32[4,136,128]{2,1,0:T(8,128)S(1)} %all_to_all.22.parts_ref, bf16[2048,2048]{1,0:T(8,128)(2,1)S(1)} %collective-permute-done.3.weight_ref), custom_call_target="tpu_custom_call" | custom-call | flops 67108864 | bytes 8388608 | tf_op jit(solution)/shard_map/pallas_call | solution.py:341
  47.2 0.0 collective-permute-start.4
  47.3 1.2 %collective-permute-done.4.second_ref = f32[128,128]{1,0:T(8,128)S(1)} collective-permute-done((f32[128,128]{1,0:T(8,128)S(1)}, f32[128,128]{1,0:T(8,128)S(1)}, u32[]{:S(2)}, u32[]{:S(2)}) %collective-permute-start.4) | collective-permute-done | bytes 65568 | tf_op jit(solution)/shard_map/ppermute | solution.py:269
  48.5 9.1 %all_to_all.23 = bf16[8,16,128]{2,1,0:T(8,128)(2,1)S(1)} all-to-all(bf16[8,16,128]{2,1,0:T(8,128)(2,1)S(1)} %bitcast.13), channel_id=1, replica_groups=mesh['parts'=2,'kv'=2,'req'=8] {'req'}, dimensions={0} | all-to-all | bytes 65536 | tf_op jit(solution)/shard_map/all_to_all | solution.py:350
  57.6 0.6 %reshape.23 = bf16[1,16384]{1,0:T(2,128)(2,1)} reshape(bf16[8,16,128]{2,1,0:T(8,128)(2,1)S(1)} %all_to_all.23) | data formatting | bytes 65536 | tf_op jit(solution)/shard_map/reshape | solution.py:353
  (5 shorter events, 0.1 us)
Async XLA Ops:
  0.0 46.0 %collective-permute-start.3 = (bf16[2048,2048]{1,0:T(8,128)(2,1)}, bf16[2048,2048]{1,0:T(8,128)(2,1)S(1)}, u32[]{:S(2)}, u32[]{:S(2)}) collective-permute-start(bf16[2048,2048]{1,0:T(8,128)(2,1)} %bitcast.16), channel_id=1, source_target_pairs={{0,8},{8,0},{1,9},{9,1},{2,10},{10,2},{3,11},{11,3},{4,12},{12,4},... | collective-permute-start | bytes 25165832 | tf_op jit(solution)/shard_map/ppermute | solution.py:269
  0.5 0.8 %copy-start.3 = (bf16[1,16384]{1,0:T(2,128)(2,1)S(1)}, bf16[1,16384]{1,0:T(2,128)(2,1)}, u32[]{:S(2)}) copy-start(bf16[1,16384]{1,0:T(2,128)(2,1)} %hidden_ref.1) | copy-start | bytes 98308
  1.3 24.4 %slice-start = ((s8[6291456]{0:T(1024)(128)(4,1)}), s8[4194304]{0:T(1024)(128)(4,1)S(1)}, s32[]{:S(2)}) async-start(s8[6291456]{0:T(1024)(128)(4,1)} %bitcast.7), calls=%async_computation.4 | async-start | bytes 8388608
  1.3 14.0 %copy-start = (bf16[2048,1,2048]{2,0,1:T(8,128)(2,1)S(1)}, bf16[2048,1,2048]{2,0,1:T(8,128)(2,1)}, u32[]{:S(2)}) copy-start(bf16[2048,1,2048]{2,0,1:T(8,128)(2,1)} %param.11) | copy-start | bytes 25165828
  1.4 13.9 %copy-start.1 = (bf16[2048,1,256]{2,0,1:T(8,128)(2,1)S(1)}, bf16[2048,1,256]{2,0,1:T(8,128)(2,1)}, u32[]{:S(2)}) copy-start(bf16[2048,1,256]{2,0,1:T(8,128)(2,1)} %param.12) | copy-start | bytes 3145732
  1.4 13.9 %copy-start.2 = (f32[16384]{0:T(1024)S(1)}, f32[16384]{0:T(1024)}, u32[]{:S(2)}) copy-start(f32[16384]{0:T(1024)} %param.10) | copy-start | bytes 196612
  1.4 24.3 %slice-start.1 = ((s8[6291456]{0:T(1024)(128)(4,1)}), s8[2097152]{0:T(1024)(128)(4,1)S(1)}, s32[]{:S(2)}) async-start(s8[6291456]{0:T(1024)(128)(4,1)} %bitcast.7), calls=%async_computation.5 | async-start | bytes 4194304
  15.3 11.3 %copy-start.4 = (s32[24]{0:T(128)S(1)}, s32[24]{0:T(128)}, u32[]{:S(2)}) copy-start(s32[24]{0:T(128)} %owner_ref.1) | copy-start | bytes 292
  15.3 11.3 %copy-start.5 = (s32[24]{0:T(128)S(1)}, s32[24]{0:T(128)}, u32[]{:S(2)}) copy-start(s32[24]{0:T(128)} %block_ref.1) | copy-start | bytes 292
  15.3 11.3 %copy-start.6 = (s32[8]{0:T(128)S(1)}, s32[8]{0:T(128)}, u32[]{:S(2)}) copy-start(s32[8]{0:T(128)} %length_ref.1) | copy-start | bytes 100
  25.2 6.0 %collective-permute-start = (f32[8,2176]{1,0:T(8,128)S(1)}, f32[8,2176]{1,0:T(8,128)S(1)}, u32[]{:S(2)}, u32[]{:S(2)}) collective-permute-start(f32[8,2176]{1,0:T(8,128)S(1)} %shard_map.95.first_ref), channel_id=1, source_target_pairs={{0,4},{1,5},{2,6},{3,7},{4,0},{5,1},{6,2},{7,3},{8,12},{9,13},{10,... | collective-permute-start | bytes 208904 | tf_op jit(solution)/shard_map/ppermute | solution.py:221
  32.6 4.8 %collective-permute-start.2 = (f32[136,128]{1,0:T(8,128)S(1)}, f32[136,128]{1,0:T(8,128)S(1)}, u32[]{:S(2)}, u32[]{:S(2)}) collective-permute-start(f32[136,128]{1,0:T(8,128)S(1)} %shard_map.97), channel_id=1, source_target_pairs={{0,12},{1,13},{2,14},{3,15},{4,8},{5,9},{6,10},{7,11},{8,4},{9,5},... | collective-permute-start | bytes 208904 | tf_op jit(solution)/shard_map/ppermute | solution.py:307
  32.7 4.8 %collective-permute-start.1 = (f32[136,128]{1,0:T(8,128)S(1)}, f32[136,128]{1,0:T(8,128)S(1)}, u32[]{:S(2)}, u32[]{:S(2)}) collective-permute-start(f32[136,128]{1,0:T(8,128)S(1)} %shard_map.97), channel_id=1, source_target_pairs={{0,8},{8,0},{1,9},{9,1},{2,10},{10,2},{3,11},{11,3},{4,12},{12,4},... | collective-permute-start | bytes 208904 | tf_op jit(solution)/shard_map/ppermute | solution.py:269
  47.2 1.3 %collective-permute-start.4 = (f32[128,128]{1,0:T(8,128)S(1)}, f32[128,128]{1,0:T(8,128)S(1)}, u32[]{:S(2)}, u32[]{:S(2)}) collective-permute-start(f32[128,128]{1,0:T(8,128)S(1)} %shard_map.99.first_ref), channel_id=1, source_target_pairs={{0,8},{8,0},{1,9},{9,1},{2,10},{10,2},{3,11},{11,3},{4,12},{12,4},... | collective-permute-start | bytes 196616 | tf_op jit(solution)/shard_map/ppermute | solution.py:269

commit v7 on v6

--- a/solution.py
+++ b/solution.py
@@ -34,7 +34,7 @@
     x = x_ref[...] * gain[None]
     x = jnp.concatenate([x[:, chunk, :] for chunk in range(chunks)], axis=1).astype(BF16)
     width = query_ref.shape[1]
-    step = 1024
+    step = width
     for at in range(0, width, step):
         y = jnp.dot(x, query_ref[:, at : at + step], preferred_element_type=F32)
         for copy in range(out_ref.shape[0]):
@@ -193,7 +193,7 @@
     ).astype(BF16)
     width = weight_ref.shape[1]
     chunks = width // LANES
-    step = min(1024, width)
+    step = width
     for at in range(0, width, step):
         y = jnp.dot(x, weight_ref[:, at : at + step], preferred_element_type=F32)
         for chunk in range(step // LANES):

time: 58.5 us -> 58.6 us (level)
  no operation moved by 1% of the time
where the time goes in v7:
time: 58.6 us; the launch traced here: 58.3 us
  blocking collectives  39.9 us (68%)
  waiting for transfers between devices  9.86 us (17%)
  Pallas kernels  5.74 us (10%)
  local copies, waits for them, and re-layouts  1.53 us (3%)
  starting transfers between devices  1.14 us (2%)
    all_to_all x1, blocking collectives, on_device(): lax.all_to_all(scaled.reshape(requests, feature_rows // LANES, LANES), 'r...  13.8 us
    all_to_all x1, blocking collectives, on_device(): lax.all_to_all(total.reshape(requests, columns_out // LANES, LANES), 'req...  9.12 us
    all_to_all x1, blocking collectives, far_then_near(): return lax.all_to_all(x, 'req', 0, 0, tiled=True, axis_index_groups=groups)  8.48 us
    all_to_all x1, blocking collectives, on_device(): lax.all_to_all(sums, 'req', 0, 0, tiled=True, axis_index_groups=groups)  8.47 us
    ppermute x1, waiting for transfers between devices, crossed(): return lax.ppermute(x, ('kv', 'req'), pairs)  4.68 us
    ppermute x1, waiting for transfers between devices, exchanged(): lax.ppermute(x, 'req', [(place, place ^ distance) for place in range(size)])  3.92 us
    pallas_call x1, Pallas kernels, attend(): call(attend_kernel, (dim + 8, rows), F32, [VMEM] * 7, [pltpu.VMEM((rows,...  1.39 us
    pallas_call x1, Pallas kernels, on_device(): call(project_kernel, (near, requests, head_width + dim), F32, [VMEM] * 4,...  1.34 us
  transfers between devices with their start and end apart: 5, of which 3 were waited for; matrix products, arithmetic and copies ran while one was open for 0% of the time, Pallas kernels for 8%

profile of v7, /device:TPU:0, one launch (start us, length us, event | category | flops | bytes accessed | tf_op | source)
XLA Modules:
  0.0 58.3 jit_solution(15480226040118365395)
XLA Ops:
  0.0 0.5 collective-permute-start.3
  0.5 0.0 copy-start.3
  0.5 0.8 %copy-done.3 = bf16[1,16384]{1,0:T(2,128)(2,1)S(1)} copy-done((bf16[1,16384]{1,0:T(2,128)(2,1)S(1)}, bf16[1,16384]{1,0:T(2,128)(2,1)}, u32[]{:S(2)}) %copy-start.3) | copy-done | bytes 32792
  1.3 0.0 slice-start
  1.3 0.0 copy-start
  1.4 0.0 copy-start.1
  1.4 0.0 copy-start.2
  1.4 0.0 slice-start.1
  1.4 0.1 shard_map.93
  1.5 13.8 %all_to_all.20.x_ref = f32[8,16,128]{2,1,0:T(8,128)S(1)} all-to-all(f32[8,16,128]{2,1,0:T(8,128)S(1)} %bitcast.15), channel_id=1, replica_groups=mesh['parts'=2,'kv'=2,'req'=8] {'req'}, dimensions={0} | all-to-all | bytes 131072 | tf_op jit(solution)/shard_map/all_to_all | solution.py:288
  15.3 0.0 copy-done
  15.3 0.0 copy-done.1
  15.3 0.0 copy-done.2
  15.3 0.0 copy-start.4
  15.3 0.0 copy-start.5
  15.3 0.0 copy-start.6
  15.3 1.3 %shard_map.94 = f32[4,8,2176]{2,1,0:T(8,128)S(1)} custom-call(f32[8,16,128]{2,1,0:T(8,128)S(1)} %all_to_all.20.x_ref, f32[128,128]{1,0:T(8,128)S(1)} %bitcast.14, bf16[2048,2048]{1,0:T(8,128)(2,1)S(1)} %bitcast.11, bf16[2048,256]{1,0:T(8,128)(2,1)S(1)} %bitcast.12), custom_call_target="tpu_custom_call" | custom-call | flops 75497472 | bytes 9437184 | tf_op jit(solution)/shard_map/pallas_call | solution.py:293
  16.7 8.5 %all_to_all.21.parts_ref = f32[4,8,2176]{2,1,0:T(8,128)S(1)} all-to-all(f32[4,8,2176]{2,1,0:T(8,128)S(1)} %shard_map.94), channel_id=1, replica_groups={{0,1,2,3},{4,5,6,7},{8,9,10,11},{12,13,14,15},{16,17,18,19},{20,21,22,2..., dimensions={0} | all-to-all | bytes 557056 | tf_op jit(solution)/shard_map/all_to_all | solution.py:325
  25.2 0.5 collective-permute-start
  25.7 0.0 slice-done
  25.7 0.0 slice-done.1
  25.7 0.9 %shard_map.96.key_ref = bf16[24,128,512]{2,1,0:T(8,128)(2,1)S(1)} custom-call(bf16[24,512,256]{2,1,0:T(8,128)(2,1)S(1)} %bitcast.9), custom_call_target="tpu_custom_call" | custom-call | bytes 6291456 | tf_op jit(solution)/shard_map/pallas_call | solution.py:241
  26.6 0.0 copy-done.4
  26.6 0.0 copy-done.5
  26.6 0.0 copy-done.6
  26.6 0.6 %shard_map.91 = (s32[8,128]{1,0:T(8,128)S(1)}, bf16[384,128]{1,0:T(8,128)(2,1)S(1)}, s32[384,128]{1,0:T(8,128)S(1)}) custom-call(s32[24]{0:T(128)S(1)} %copy-done.4, s32[24]{0:T(128)S(1)} %copy-done.5, s32[8]{0:T(128)S(1)} %copy-done.6), custom_call_target="tpu_custom_call" | custom-call | tf_op jit(solution)/shard_map/pallas_call | solution.py:226
  27.3 3.9 %collective-permute-done.second_ref = f32[8,2176]{1,0:T(8,128)S(1)} collective-permute-done((f32[8,2176]{1,0:T(8,128)S(1)}, f32[8,2176]{1,0:T(8,128)S(1)}, u32[]{:S(2)}, u32[]{:S(2)}) %collective-permute-start) | collective-permute-done | bytes 69664 | tf_op jit(solution)/shard_map/ppermute | solution.py:221
  31.2 1.4 %shard_map.97 = f32[136,128]{1,0:T(8,128)S(1)} custom-call(s32[8,128]{1,0:T(8,128)S(1)} %get-tuple-element.8.place_ref, bf16[384,128]{1,0:T(8,128)(2,1)S(1)} %get-tuple-element.9.pick_ref, s32[384,128]{1,0:T(8,128)S(1)} %get-tuple-element.10.live_ref, f32[8,2176]{1,0:T(8,128)S(1)} %shard_map.95.first_ref, f32[8,2176]{1,0:T(8,128)S(1)} %collective-permute-done.second_ref, ...), custom_call_target="tpu_custom_call" | custom-call | flops 100663296 | bytes 6291456 | tf_op jit(solution)/shard_map/pallas_call | solution.py:252
  32.6 0.1 collective-permute-start.2
  32.7 0.1 collective-permute-start.1
  32.7 4.7 %collective-permute-done.2.second_ref = f32[136,128]{1,0:T(8,128)S(1)} collective-permute-done((f32[136,128]{1,0:T(8,128)S(1)}, f32[136,128]{1,0:T(8,128)S(1)}, u32[]{:S(2)}, u32[]{:S(2)}) %collective-permute-start.2) | collective-permute-done | bytes 69664 | tf_op jit(solution)/shard_map/ppermute | solution.py:307
  37.4 0.0 collective-permute-done.1.first_ref
  37.5 8.5 %all_to_all.22.parts_ref = f32[4,136,128]{2,1,0:T(8,128)S(1)} all-to-all(f32[4,136,128]{2,1,0:T(8,128)S(1)} %shard_map.98), channel_id=1, replica_groups={{0,1,2,3},{4,5,6,7},{8,9,10,11},{12,13,14,15},{16,17,18,19},{20,21,22,2..., dimensions={0} | all-to-all | bytes 557056 | tf_op jit(solution)/shard_map/all_to_all | solution.py:319
  45.9 0.0 collective-permute-done.3.weight_ref
  45.9 1.3 %shard_map.99.first_ref = f32[128,128]{1,0:T(8,128)S(1)} custom-call(f32[4,136,128]{2,1,0:T(8,128)S(1)} %all_to_all.22.parts_ref, bf16[2048,2048]{1,0:T(8,128)(2,1)S(1)} %collective-permute-done.3.weight_ref), custom_call_target="tpu_custom_call" | custom-call | flops 67108864 | bytes 8388608 | tf_op jit(solution)/shard_map/pallas_call | solution.py:341
  47.2 0.0 collective-permute-start.4
  47.3 1.2 %collective-permute-done.4.second_ref = f32[128,128]{1,0:T(8,128)S(1)} collective-permute-done((f32[128,128]{1,0:T(8,128)S(1)}, f32[128,128]{1,0:T(8,128)S(1)}, u32[]{:S(2)}, u32[]{:S(2)}) %collective-permute-start.4) | collective-permute-done | bytes 65568 | tf_op jit(solution)/shard_map/ppermute | solution.py:269
  48.5 9.1 %all_to_all.23 = bf16[8,16,128]{2,1,0:T(8,128)(2,1)S(1)} all-to-all(bf16[8,16,128]{2,1,0:T(8,128)(2,1)S(1)} %bitcast.13), channel_id=1, replica_groups=mesh['parts'=2,'kv'=2,'req'=8] {'req'}, dimensions={0} | all-to-all | bytes 65536 | tf_op jit(solution)/shard_map/all_to_all | solution.py:350
  57.6 0.6 %reshape.23 = bf16[1,16384]{1,0:T(2,128)(2,1)} reshape(bf16[8,16,128]{2,1,0:T(8,128)(2,1)S(1)} %all_to_all.23) | data formatting | bytes 65536 | tf_op jit(solution)/shard_map/reshape | solution.py:353
  (5 shorter events, 0.1 us)
Async XLA Ops:
  0.0 45.9 %collective-permute-start.3 = (bf16[2048,2048]{1,0:T(8,128)(2,1)}, bf16[2048,2048]{1,0:T(8,128)(2,1)S(1)}, u32[]{:S(2)}, u32[]{:S(2)}) collective-permute-start(bf16[2048,2048]{1,0:T(8,128)(2,1)} %bitcast.16), channel_id=1, source_target_pairs={{0,8},{8,0},{1,9},{9,1},{2,10},{10,2},{3,11},{11,3},{4,12},{12,4},... | collective-permute-start | bytes 25165832 | tf_op jit(solution)/shard_map/ppermute | solution.py:269
  0.5 0.8 %copy-start.3 = (bf16[1,16384]{1,0:T(2,128)(2,1)S(1)}, bf16[1,16384]{1,0:T(2,128)(2,1)}, u32[]{:S(2)}) copy-start(bf16[1,16384]{1,0:T(2,128)(2,1)} %hidden_ref.1) | copy-start | bytes 98308
  1.3 24.4 %slice-start = ((s8[6291456]{0:T(1024)(128)(4,1)}), s8[4194304]{0:T(1024)(128)(4,1)S(1)}, s32[]{:S(2)}) async-start(s8[6291456]{0:T(1024)(128)(4,1)} %bitcast.7), calls=%async_computation.4 | async-start | bytes 8388608
  1.3 14.0 %copy-start = (bf16[2048,1,2048]{2,0,1:T(8,128)(2,1)S(1)}, bf16[2048,1,2048]{2,0,1:T(8,128)(2,1)}, u32[]{:S(2)}) copy-start(bf16[2048,1,2048]{2,0,1:T(8,128)(2,1)} %param.11) | copy-start | bytes 25165828
  1.4 13.9 %copy-start.1 = (bf16[2048,1,256]{2,0,1:T(8,128)(2,1)S(1)}, bf16[2048,1,256]{2,0,1:T(8,128)(2,1)}, u32[]{:S(2)}) copy-start(bf16[2048,1,256]{2,0,1:T(8,128)(2,1)} %param.12) | copy-start | bytes 3145732
  1.4 13.9 %copy-start.2 = (f32[16384]{0:T(1024)S(1)}, f32[16384]{0:T(1024)}, u32[]{:S(2)}) copy-start(f32[16384]{0:T(1024)} %param.10) | copy-start | bytes 196612
  1.4 24.3 %slice-start.1 = ((s8[6291456]{0:T(1024)(128)(4,1)}), s8[2097152]{0:T(1024)(128)(4,1)S(1)}, s32[]{:S(2)}) async-start(s8[6291456]{0:T(1024)(128)(4,1)} %bitcast.7), calls=%async_computation.5 | async-start | bytes 4194304
  15.3 11.3 %copy-start.4 = (s32[24]{0:T(128)S(1)}, s32[24]{0:T(128)}, u32[]{:S(2)}) copy-start(s32[24]{0:T(128)} %owner_ref.1) | copy-start | bytes 292
  15.3 11.3 %copy-start.5 = (s32[24]{0:T(128)S(1)}, s32[24]{0:T(128)}, u32[]{:S(2)}) copy-start(s32[24]{0:T(128)} %block_ref.1) | copy-start | bytes 292
  15.3 11.3 %copy-start.6 = (s32[8]{0:T(128)S(1)}, s32[8]{0:T(128)}, u32[]{:S(2)}) copy-start(s32[8]{0:T(128)} %length_ref.1) | copy-start | bytes 100
  25.2 6.0 %collective-permute-start = (f32[8,2176]{1,0:T(8,128)S(1)}, f32[8,2176]{1,0:T(8,128)S(1)}, u32[]{:S(2)}, u32[]{:S(2)}) collective-permute-start(f32[8,2176]{1,0:T(8,128)S(1)} %shard_map.95.first_ref), channel_id=1, source_target_pairs={{0,4},{1,5},{2,6},{3,7},{4,0},{5,1},{6,2},{7,3},{8,12},{9,13},{10,... | collective-permute-start | bytes 208904 | tf_op jit(solution)/shard_map/ppermute | solution.py:221
  32.6 4.8 %collective-permute-start.2 = (f32[136,128]{1,0:T(8,128)S(1)}, f32[136,128]{1,0:T(8,128)S(1)}, u32[]{:S(2)}, u32[]{:S(2)}) collective-permute-start(f32[136,128]{1,0:T(8,128)S(1)} %shard_map.97), channel_id=1, source_target_pairs={{0,12},{1,13},{2,14},{3,15},{4,8},{5,9},{6,10},{7,11},{8,4},{9,5},... | collective-permute-start | bytes 208904 | tf_op jit(solution)/shard_map/ppermute | solution.py:307
  32.7 4.8 %collective-permute-start.1 = (f32[136,128]{1,0:T(8,128)S(1)}, f32[136,128]{1,0:T(8,128)S(1)}, u32[]{:S(2)}, u32[]{:S(2)}) collective-permute-start(f32[136,128]{1,0:T(8,128)S(1)} %shard_map.97), channel_id=1, source_target_pairs={{0,8},{8,0},{1,9},{9,1},{2,10},{10,2},{3,11},{11,3},{4,12},{12,4},... | collective-permute-start | bytes 208904 | tf_op jit(solution)/shard_map/ppermute | solution.py:269
  47.2 1.3 %collective-permute-start.4 = (f32[128,128]{1,0:T(8,128)S(1)}, f32[128,128]{1,0:T(8,128)S(1)}, u32[]{:S(2)}, u32[]{:S(2)}) collective-permute-start(f32[128,128]{1,0:T(8,128)S(1)} %shard_map.99.first_ref), channel_id=1, source_target_pairs={{0,8},{8,0},{1,9},{9,1},{2,10},{10,2},{3,11},{11,3},{4,12},{12,4},... | collective-permute-start | bytes 196616 | tf_op jit(solution)/shard_map/ppermute | solution.py:269
